TPU v7x, 128 devices: a whole 4x4x4 slice. The times are simulated.
128 devices in a mesh: lat: 32 (over x, y, core), ch: 4 (over z).
Axes of the slice: x: 4, y: 4, z: 4, core: 2. Of those that a mesh axis runs over, the one named last changes fastest.
Arguments:
- state: float32 [128, 256, 1024], P('lat', None, 'ch'), may hold values from -6 to 6
- residual: float32 [128, 256, 1024], P('lat', None, 'ch'), may hold values from -6 to 6
- direction: float32 [128, 256, 1024], P('lat', None, 'ch'), may hold values from -6 to 6
- precond: float32 [128, 256, 1024], P('lat', None, 'ch'), may hold values from 0.5 to 4
- token_slope: bfloat16 [32768, 4096], P('lat', 'ch'), may hold values from -0.099609375 to 1.09375
- spectral_slope: bfloat16 [2, 128, 128, 1024], P(None, None, 'lat', 'ch'), may hold values from -0.099609375 to 1.09375
- filter_in: float32 [2, 8, 128, 128], P(None, 'ch'), may hold values from -0.375 to 0.375
- filter_out: float32 [2, 8, 128, 128], P(None, 'ch'), may hold values from -0.375 to 0.375
- w_up: bfloat16 [1024, 4096], P(None, 'ch'), may hold values from -0.1875 to 0.1875
- w_down: bfloat16 [4096, 1024], P('ch'), may hold values from -0.09375 to 0.09375
- obs_weight: float32 [1024], P('ch'), may hold values from -0.6 to 0.6
- obs_token: int32 [32, 4, 128], P('lat'), may hold values from 0 to 32767
- obs_count: int32 [32, 4], P('lat'), may hold values from 1 to 128, 320 in all within a row
- obs_rinv: float32 [32, 4, 128], P('lat'), may hold values from 1 to 10
Outputs:
- state_next: float32 [128, 256, 1024], P('lat', None, 'ch')
- residual_next: float32 [128, 256, 1024], P('lat', None, 'ch')
- direction_next: float32 [128, 256, 1024], P('lat', None, 'ch')
Inputs may be any that keep to these rules, and one draw needn't show every extreme that they name: `obs_count`: in every latitude band the 4 counts sum to 320, and the largest is 128.
All inputs are finite; a program needn't handle non-finite values.
Results may differ from a plain program's by a relative error of at most 0.015.
Values may be sent and summed in bfloat16 or wider, within the bound.
A program may use at most 128 MiB of HBM per device.

v0:
```python
import math

import jax
import jax.numpy as jnp
from jax import lax
from jax.sharding import PartitionSpec as P

HIGH = lax.Precision.HIGHEST


def tables(length, count):
    freq = lax.broadcasted_iota(jnp.int32, (count, length), 0)
    place = lax.broadcasted_iota(jnp.int32, (count, length), 1)
    angle = 2.0 * math.pi / length * (freq * place % length).astype(jnp.float32)
    return (jnp.cos(angle), jnp.sin(angle))


def spectral_tables(width, height):
    lon_cos, lon_sin = tables(width, width // 2)
    wave = lax.broadcasted_iota(jnp.int32, (width // 2, 1), 0)
    factor = jnp.where(wave == 0, jnp.float32(1.0), jnp.float32(2.0)) / width
    lat_cos, lat_sin = tables(height, height)
    return (lon_cos, lon_sin, lon_cos * factor, lon_sin * factor, lat_cos, lat_sin)


def lon_forward(field, cos_table, sin_table):
    real_part = jnp.einsum("kw,lwd->lkd", cos_table, field, precision=HIGH)
    imag_part = -jnp.einsum("kw,lwd->lkd", sin_table, field, precision=HIGH)
    return (real_part, imag_part)


def lon_backward(real_part, imag_part, cos_table, sin_table):
    first_term = jnp.einsum("kw,lkd->lwd", cos_table, real_part, precision=HIGH)
    return first_term - jnp.einsum("kw,lkd->lwd", sin_table, imag_part, precision=HIGH)


def lat_mix(real_part, imag_part, cos_table, sin_table, sign):
    cos_real = jnp.einsum("mh,hkd->mkd", cos_table, real_part, precision=HIGH)
    cos_imag = jnp.einsum("mh,hkd->mkd", cos_table, imag_part, precision=HIGH)
    sin_real = jnp.einsum("mh,hkd->mkd", sin_table, real_part, precision=HIGH)
    sin_imag = jnp.einsum("mh,hkd->mkd", sin_table, imag_part, precision=HIGH)
    return (cos_real + sign * sin_imag, cos_imag - sign * sin_real)


def block_product(real_part, imag_part, weights, flip):
    lead = real_part.shape[:-1]
    blocks = weights.shape[1]
    width = weights.shape[2]
    real_blocks = real_part.reshape(lead + (blocks, width))
    imag_blocks = imag_part.reshape(lead + (blocks, width))
    if flip:
        form = "hknc,nbc->hknb"
        other = -weights[1]
    else:
        form = "hknb,nbc->hknc"
        other = weights[1]
    new_real = jnp.einsum(form, real_blocks, weights[0], precision=HIGH) - jnp.einsum(
        form, imag_blocks, other, precision=HIGH
    )
    new_imag = jnp.einsum(form, real_blocks, other, precision=HIGH) + jnp.einsum(
        form, imag_blocks, weights[0], precision=HIGH
    )
    return (new_real.reshape(lead + (blocks * width,)), new_imag.reshape(lead + (blocks * width,)))


def spectral(field, slope, first, second, tabs, flip):
    lon_cos, lon_sin, inv_cos, inv_sin, lat_cos, lat_sin = tabs
    if flip:
        real_part, imag_part = lon_forward(field, inv_cos, inv_sin)
    else:
        real_part, imag_part = lon_forward(field, lon_cos, lon_sin)
    real_part, imag_part = (
        lax.all_to_all(
            real_part.astype(jnp.bfloat16), "lat", split_axis=1, concat_axis=0, tiled=True
        ).astype(real_part.dtype),
        lax.all_to_all(
            imag_part.astype(jnp.bfloat16), "lat", split_axis=1, concat_axis=0, tiled=True
        ).astype(imag_part.dtype),
    )
    height = lat_cos.shape[0]
    if flip:
        real_part, imag_part = lat_mix(
            real_part, imag_part, lat_cos / height, lat_sin / height, 1.0
        )
    else:
        real_part, imag_part = lat_mix(real_part, imag_part, lat_cos, lat_sin, 1.0)
    real_part, imag_part = block_product(real_part, imag_part, first, flip)
    real_part = real_part * slope[0].astype(jnp.float32)
    imag_part = imag_part * slope[1].astype(jnp.float32)
    real_part, imag_part = block_product(real_part, imag_part, second, flip)
    if flip:
        real_part, imag_part = lat_mix(real_part, imag_part, lat_cos, lat_sin, -1.0)
    else:
        real_part, imag_part = lat_mix(
            real_part, imag_part, lat_cos / height, lat_sin / height, -1.0
        )
    real_part, imag_part = (
        lax.all_to_all(
            real_part.astype(jnp.bfloat16), "lat", split_axis=0, concat_axis=1, tiled=True
        ).astype(real_part.dtype),
        lax.all_to_all(
            imag_part.astype(jnp.bfloat16), "lat", split_axis=0, concat_axis=1, tiled=True
        ).astype(imag_part.dtype),
    )
    if flip:
        return lon_backward(real_part, imag_part, lon_cos, lon_sin)
    return lon_backward(real_part, imag_part, inv_cos, inv_sin)


def product(left, right, flip):
    if flip:
        return lax.dot_general(
            left, right, (((1,), (1,)), ((), ())), preferred_element_type=jnp.float32
        )
    return jnp.dot(left, right, preferred_element_type=jnp.float32)


def mix_features(rows, first, second, slope, flip):
    lowered = rows.astype(jnp.bfloat16)
    if flip:
        part = first
    else:
        part = first
    total = product(lax.all_gather(lowered, "ch", axis=1, tiled=True), part, flip)
    hidden = (total * slope).astype(jnp.bfloat16)
    partial_terms = product(hidden, second, flip)
    return lax.psum_scatter(
        partial_terms.astype(jnp.bfloat16), "ch", scatter_dimension=1, tiled=True
    ).astype(jnp.float32)


def shards(
    state,
    residual,
    direction,
    precond,
    token_slope,
    spectral_slope,
    filter_in,
    filter_out,
    w_up,
    w_down,
    obs_weight,
    obs_token,
    obs_count,
    obs_rinv,
):
    bands, width, depth = direction.shape
    height = bands * lax.axis_size("lat")
    tabs = spectral_tables(width, height)
    norm_now = lax.psum(jnp.sum(residual * residual / precond), ("lat", "ch"))

    def token_mix(rows, flip):
        if flip:
            return mix_features(rows, w_down, w_up, token_slope, flip)
        return mix_features(rows, w_up, w_down, token_slope, flip)

    first = direction + spectral(direction, spectral_slope, filter_in, filter_out, tabs, False)
    first_rows = first.reshape(bands * width, depth)
    second_rows = first_rows + token_mix(first_rows, False)
    projected = jnp.dot(second_rows, obs_weight, precision=HIGH)
    summed = lax.psum(projected, "ch")
    whole_field = lax.all_gather(summed, "lat", axis=0, tiled=True)
    picked = whole_field[obs_token]
    slots = lax.broadcasted_iota(jnp.int32, obs_token.shape, 2)
    weighted = jnp.where(slots < obs_count[:, :, None], obs_rinv * picked, jnp.float32(0.0))
    spread = (
        jnp.zeros((height * width,), jnp.float32)
        .at[obs_token.reshape(-1)]
        .add(weighted.reshape(-1))
    )
    band_values = lax.psum_scatter(
        spread.astype(jnp.bfloat16), "lat", scatter_dimension=0, tiled=True
    ).astype(jnp.float32)
    back_rows = band_values[:, None] * obs_weight[None, :]
    back_mid_rows = back_rows + token_mix(back_rows, True)
    back_mid = back_mid_rows.reshape(bands, width, depth)
    image = (
        direction + back_mid + spectral(back_mid, spectral_slope, filter_out, filter_in, tabs, True)
    )
    curve = lax.psum(jnp.sum(direction * image), ("lat", "ch"))
    alpha = norm_now / curve
    state_next = state + alpha * direction
    residual_next = residual - alpha * image
    scaled = residual_next / precond
    norm_next = lax.psum(jnp.sum(residual_next * scaled), ("lat", "ch"))
    direction_next = scaled + norm_next / norm_now * direction
    return (state_next, residual_next, direction_next)


def solution(mesh):
    return jax.shard_map(
        shards,
        mesh=mesh,
        in_specs=(
            P("lat", None, "ch"),
            P("lat", None, "ch"),
            P("lat", None, "ch"),
            P("lat", None, "ch"),
            P("lat", "ch"),
            P(None, None, "lat", "ch"),
            P(None, "ch", None, None),
            P(None, "ch", None, None),
            P(None, "ch"),
            P("ch", None),
            P("ch"),
            P("lat", None, None),
            P("lat", None),
            P("lat", None, None),
        ),
        out_specs=(P("lat", None, "ch"), P("lat", None, "ch"), P("lat", None, "ch")),
        check_vma=False,
    )
```

profile of v0, /device:TPU:1, one launch (start us, length us, event | category | flops | bytes accessed | tf_op | source)
XLA Modules:
  0.0 617.8 jit_solution(10692976149735413343)
XLA Ops:
  10.7 8.6 %all-to-all-start = ((bf16[4,128,256]{2,0,1:T(4,128)(2,1)}), bf16[4,128,256]{2,0,1:T(4,128)(2,1)S(1)}, u32[]{:S(2)}, u32[]{:S(2)}) async-start(bf16[4,128,256]{2,0,1:T(4,128)(2,1)} %copy.113), calls=%async_computation | async-start | bytes 524288 | tf_op jit(solution)/shard_map/all_to_all | solution.py:73
  21.4 6.9 %all-to-all-done = bf16[4,128,256]{2,0,1:T(4,128)(2,1)S(1)} async-done(((bf16[4,128,256]{2,0,1:T(4,128)(2,1)}), bf16[4,128,256]{2,0,1:T(4,128)(2,1)S(1)}, u32[]{:S(2)}, u32[]{:S(2)}) %all-to-all-start) | async-done | bytes 262176 | tf_op jit(solution)/shard_map/all_to_all | solution.py:73
  28.3 5.1 all-to-all-start.1
  61.2 7.9 %all-to-all-start.2 = ((bf16[128,4,256]{2,1,0:T(4,128)(2,1)}), bf16[128,4,256]{2,1,0:T(4,128)(2,1)}, u32[]{:S(2)}, u32[]{:S(2)}) async-start(bf16[128,4,256]{2,1,0:T(4,128)(2,1)} %copy.131), calls=%async_computation.2 | async-start | bytes 524288 | tf_op jit(solution)/shard_map/all_to_all | solution.py:98
  72.1 5.9 all-to-all-done.2
  78.0 4.4 all-to-all-start.3
  85.9 5.6 all-to-all-done.3
  101.0 32.2 %all-gather.3.cloned.1.call-done = bf16[1024,1024]{1,0:T(8,128)(2,1)} async-done(((bf16[1024,256]{1,0:T(8,128)(2,1)}), bf16[1024,1024]{1,0:T(8,128)(2,1)}) %all-gather.3.cloned.1.call-update) | async-done | bytes 2097168 | tf_op jit(solution)/shard_map/all_gather | solution.py:124
  133.3 8.7 %convolution_convert_fusion.1 = bf16[1024,1024]{1,0:T(8,128)(2,1)} fusion(bf16[1024,1024]{1,0:T(8,128)(2,1)S(1)} %copy-done, bf16[1024,1024]{1,0:T(8,128)(2,1)} %param.18, bf16[1024,1024]{1,0:T(8,128)(2,1)} %all-gather.3.cloned.1.call-done, bf16[1024,1024]{1,0:T(8,128)(2,1)} %param.22), kind=kOutput, calls=%fused_computation.7 | convolution fusion | flops 4299161600 | bytes 10485760 | tf_op jit(solution)/shard_map/dot_general | solution.py:115
  143.2 30.6 %reduce-scatter.3.cloned.1.call-done = bf16[1024,256]{1,0:T(8,128)(2,1)} async-done(((bf16[1024,1024]{1,0:T(8,128)(2,1)}), bf16[1024,256]{1,0:T(8,128)(2,1)}) %reduce-scatter.3.cloned.1.call-update) | async-done | bytes 524304 | tf_op jit(solution)/shard_map/reduce_scatter | solution.py:127
  176.2 6.5 %psum.29 = f32[1024]{0:T(1024)S(1)} all-reduce(f32[1024]{0:T(1024)S(1)} %bitcast.334), channel_id=1, replica_groups=mesh['lat'=32,'ch'=4] {'ch'}, use_global_device_ids=true, to_apply=%region_3.4 | all-reduce | flops 1024 | bytes 8192 | tf_op jit(solution)/shard_map/psum | solution.py:162
  182.7 27.0 %all_gather.10 = f32[32768]{0:T(1024)S(1)} all-gather(f32[1024]{0:T(1024)S(1)} %psum.29), channel_id=1, replica_groups=mesh['lat'=32,'ch'=4] {'lat'}, dimensions={0}, use_global_device_ids=true | all-gather | bytes 135168 | tf_op jit(solution)/shard_map/all_gather | solution.py:163
  209.8 3.1 gather_fusion
  213.7 3.4 scatter_custom_fusion
  219.7 90.6 %all-reduce.4.cloned.1.call-done = bf16[32768]{0:T(1024)(128)(2,1)} async-done(((bf16[32768]{0:T(1024)(128)(2,1)}), bf16[32768]{0:T(1024)(128)(2,1)}) %all-reduce.4.cloned.1.call-update) | async-done | bytes 65552
  312.3 32.7 %all-gather.5.cloned.1.call-done = bf16[1024,1024]{1,0:T(8,128)(2,1)} async-done(((bf16[1024,256]{1,0:T(8,128)(2,1)}), bf16[1024,1024]{1,0:T(8,128)(2,1)}) %all-gather.5.cloned.1.call-update) | async-done | bytes 2097168 | tf_op jit(solution)/shard_map/all_gather | solution.py:124
  345.0 8.7 %convolution_convert_fusion = bf16[1024,1024]{1,0:T(8,128)(2,1)} fusion(bf16[1024,1024]{1,0:T(8,128)(2,1)} %param.22, bf16[1024,1024]{1,0:T(8,128)(2,1)} %param.18, bf16[1024,1024]{1,0:T(8,128)(2,1)} %all-gather.5.cloned.1.call-done, bf16[1024,1024]{1,0:T(8,128)(2,1)S(1)} %copy-done), kind=kOutput, calls=%fused_computation.6 | convolution fusion | flops 4299161600 | bytes 10485760 | tf_op jit(solution)/shard_map/dot_general | solution.py:112
  353.7 31.8 %reduce-scatter.5.cloned.1.call-done = bf16[1024,256]{1,0:T(8,128)(2,1)} async-done(((bf16[1024,1024]{1,0:T(8,128)(2,1)}), bf16[1024,256]{1,0:T(8,128)(2,1)}) %reduce-scatter.5.cloned.1.call-update) | async-done | bytes 524304 | tf_op jit(solution)/shard_map/reduce_scatter | solution.py:127
  389.9 7.5 %all-to-all-start.5 = ((bf16[4,128,256]{2,0,1:T(4,128)(2,1)}), bf16[4,128,256]{2,0,1:T(4,128)(2,1)S(1)}, u32[]{:S(2)}, u32[]{:S(2)}) async-start(bf16[4,128,256]{2,0,1:T(4,128)(2,1)} %copy.145), calls=%async_computation.7 | async-start | bytes 524288 | tf_op jit(solution)/shard_map/all_to_all | solution.py:76
  400.5 5.9 all-to-all-done.5
  406.3 4.9 all-to-all-start.4
  416.3 2.6 copy.171
  434.7 7.8 %all-to-all-start.7 = ((bf16[128,4,256]{2,1,0:T(4,128)(2,1)}), bf16[128,4,256]{2,1,0:T(4,128)(2,1)S(1)}, u32[]{:S(2)}, u32[]{:S(2)}) async-start(bf16[128,4,256]{2,1,0:T(4,128)(2,1)} %copy.166), calls=%async_computation.9 | async-start | bytes 524288 | tf_op jit(solution)/shard_map/all_to_all | solution.py:101
  445.4 6.1 all-to-all-done.7
  451.4 4.4 all-to-all-start.6
  459.6 5.3 all-to-all-done.6
  467.1 2.7 multiply_reduce_fusion.1
  469.8 62.7 %all-reduce.1 = (f32[]{:T(128)}, f32[]{:T(128)}) all-reduce(f32[]{:T(128)} %fusion.36, f32[]{:T(128)} %get-tuple-element.21), channel_id=1, replica_groups=mesh['lat'=32,'ch'=4] {'lat','ch'}, use_global_device_ids=true, to_apply=%region_1.2 | all-reduce | flops 2 | bytes 16 | tf_op jit(solution)/shard_map/psum | solution.py:151
  533.9 3.8 multiply_reduce_fusion
  537.6 62.9 %psum.31 = f32[]{:T(128)} all-reduce(f32[]{:T(128)} %get-tuple-element.14), channel_id=1, replica_groups=mesh['lat'=32,'ch'=4] {'lat','ch'}, use_global_device_ids=true, to_apply=%region_10.11 | all-reduce | flops 1 | bytes 8 | tf_op jit(solution)/shard_map/psum | solution.py:186
  601.8 2.8 multiply_add_fusion.1
  607.1 2.7 copy.177
  (151 shorter events, 98.3 us)
Async XLA Ops:
  7.2 126.1 %copy-start = (bf16[1024,1024]{1,0:T(8,128)(2,1)S(1)}, bf16[1024,1024]{1,0:T(8,128)(2,1)}, u32[]{:S(2)}) copy-start(bf16[1024,1024]{1,0:T(8,128)(2,1)} %param.23) | copy-start | bytes 6291460
  7.2 12.1 %copy-start.2 = (f32[4,256,256]{2,1,0:T(8,128)S(1)}, f32[4,256,256]{2,1,0:T(8,128)}, u32[]{:S(2)}) copy-start(f32[4,256,256]{2,1,0:T(8,128)} %param.16) | copy-start | bytes 3145732
  10.7 17.6 %all-to-all-start = ((bf16[4,128,256]{2,0,1:T(4,128)(2,1)}), bf16[4,128,256]{2,0,1:T(4,128)(2,1)S(1)}, u32[]{:S(2)}, u32[]{:S(2)}) async-start(bf16[4,128,256]{2,0,1:T(4,128)(2,1)} %copy.113), calls=%async_computation | async-start | bytes 524288 | tf_op jit(solution)/shard_map/all_to_all | solution.py:73
  28.3 7.1 %copy-start.17 = (bf16[4,128,256]{2,0,1:T(4,128)(2,1)}, bf16[4,128,256]{2,0,1:T(4,128)(2,1)S(1)}, u32[]{:S(2)}) copy-start(bf16[4,128,256]{2,0,1:T(4,128)(2,1)S(1)} %all-to-all-done) | copy-start | bytes 786436
  28.3 15.5 %all-to-all-start.1 = ((bf16[4,128,256]{2,0,1:T(4,128)(2,1)}), bf16[4,128,256]{2,0,1:T(4,128)(2,1)}, u32[]{:S(2)}, u32[]{:S(2)}) async-start(bf16[4,128,256]{2,0,1:T(4,128)(2,1)} %copy.115), calls=%async_computation.1 | async-start | bytes 524288 | tf_op jit(solution)/shard_map/all_to_all | solution.py:76
  41.4 9.2 %copy-start.10 = (f32[2,2,128,128]{3,2,1,0:T(8,128)S(1)}, f32[2,2,128,128]{3,2,1,0:T(8,128)}, u32[]{:S(2)}) copy-start(f32[2,2,128,128]{3,2,1,0:T(8,128)} %param.20) | copy-start | bytes 786436
  47.2 4.5 copy-start.14
  52.3 1.9 copy-start.4
  61.2 16.8 %all-to-all-start.2 = ((bf16[128,4,256]{2,1,0:T(4,128)(2,1)}), bf16[128,4,256]{2,1,0:T(4,128)(2,1)}, u32[]{:S(2)}, u32[]{:S(2)}) async-start(bf16[128,4,256]{2,1,0:T(4,128)(2,1)} %copy.131), calls=%async_computation.2 | async-start | bytes 524288 | tf_op jit(solution)/shard_map/all_to_all | solution.py:98
  78.0 13.5 %all-to-all-start.3 = ((bf16[128,4,256]{2,1,0:T(4,128)(2,1)}), bf16[128,4,256]{2,1,0:T(4,128)(2,1)}, u32[]{:S(2)}, u32[]{:S(2)}) async-start(bf16[128,4,256]{2,1,0:T(4,128)(2,1)} %copy.136), calls=%async_computation.3 | async-start | bytes 524288 | tf_op jit(solution)/shard_map/all_to_all | solution.py:101
  82.4 50.9 %all-gather.3.cloned.1.call-start = ((), (), s32[]{:S(2)}) async-start(), calls=%async_computation.10 | async-start | bytes 2621440 | tf_op jit(solution)/shard_map/all_gather | solution.py:124
  101.0 72.8 %reduce-scatter.3.cloned.1.call-start = ((), (), s32[]{:S(2)}) async-start(), calls=%async_computation.11 | async-start | bytes 2621440 | tf_op jit(solution)/shard_map/reduce_scatter | solution.py:127
  142.0 33.3 %copy-start.21 = (f32[256]{0:T(256)S(1)}, f32[256]{0:T(256)}, u32[]{:S(2)}) copy-start(f32[256]{0:T(256)} %param.24) | copy-start | bytes 3076
  142.0 168.3 %all-reduce.4.cloned.1.call-start = ((), (), s32[]{:S(2)}) async-start(), calls=%async_computation.14 | async-start | bytes 131072
  217.8 127.2 %all-gather.5.cloned.1.call-start = ((), (), s32[]{:S(2)}) async-start(), calls=%async_computation.12 | async-start | bytes 2621440 | tf_op jit(solution)/shard_map/all_gather | solution.py:124
  312.0 73.5 %reduce-scatter.5.cloned.1.call-start = ((), (), s32[]{:S(2)}) async-start(), calls=%async_computation.13 | async-start | bytes 2621440 | tf_op jit(solution)/shard_map/reduce_scatter | solution.py:127
  389.9 16.5 %all-to-all-start.5 = ((bf16[4,128,256]{2,0,1:T(4,128)(2,1)}), bf16[4,128,256]{2,0,1:T(4,128)(2,1)S(1)}, u32[]{:S(2)}, u32[]{:S(2)}) async-start(bf16[4,128,256]{2,0,1:T(4,128)(2,1)} %copy.145), calls=%async_computation.7 | async-start | bytes 524288 | tf_op jit(solution)/shard_map/all_to_all | solution.py:76
  397.4 14.3 %slice-start = ((f32[2,2,128,128]{3,2,1,0:T(8,128)}), f32[1,2,128,128]{3,2,1,0:T(8,128)S(1)}, s32[]{:S(2)}) async-start(f32[2,2,128,128]{3,2,1,0:T(8,128)} %param.21), calls=%async_computation.15 | async-start | bytes 262144 | tf_op jit(solution)/shard_map/slice | solution.py:56
  406.3 5.0 copy-start.18
  406.3 14.1 %all-to-all-start.4 = ((bf16[4,128,256]{2,0,1:T(4,128)(2,1)}), bf16[4,128,256]{2,0,1:T(4,128)(2,1)}, u32[]{:S(2)}, u32[]{:S(2)}) async-start(bf16[4,128,256]{2,0,1:T(4,128)(2,1)} %copy.142), calls=%async_computation.6 | async-start | bytes 524288 | tf_op jit(solution)/shard_map/all_to_all | solution.py:73
  411.7 3.3 copy-start.9
  416.3 2.6 copy-start.19
  419.0 2.5 copy-start.15
  421.6 3.9 copy-start.13
  421.6 4.5 copy-start.16
  423.8 2.8 copy-start.7
  426.7 1.8 copy-start.5
  434.7 16.7 %all-to-all-start.7 = ((bf16[128,4,256]{2,1,0:T(4,128)(2,1)}), bf16[128,4,256]{2,1,0:T(4,128)(2,1)S(1)}, u32[]{:S(2)}, u32[]{:S(2)}) async-start(bf16[128,4,256]{2,1,0:T(4,128)(2,1)} %copy.166), calls=%async_computation.9 | async-start | bytes 524288 | tf_op jit(solution)/shard_map/all_to_all | solution.py:101
  451.4 7.2 %copy-start.20 = (bf16[128,4,256]{2,1,0:T(4,128)(2,1)}, bf16[128,4,256]{2,1,0:T(4,128)(2,1)S(1)}, u32[]{:S(2)}) copy-start(bf16[128,4,256]{2,1,0:T(4,128)(2,1)S(1)} %all-to-all-done.7) | copy-start | bytes 786436
  451.4 13.5 %all-to-all-start.6 = ((bf16[128,4,256]{2,1,0:T(4,128)(2,1)}), bf16[128,4,256]{2,1,0:T(4,128)(2,1)}, u32[]{:S(2)}, u32[]{:S(2)}) async-start(bf16[128,4,256]{2,1,0:T(4,128)(2,1)} %copy.161), calls=%async_computation.8 | async-start | bytes 524288 | tf_op jit(solution)/shard_map/all_to_all | solution.py:98
  533.8 68.0 %copy-start.11 = (f32[4,256,256]{1,2,0:T(8,128)S(1)}, f32[4,256,256]{1,2,0:T(8,128)}, u32[]{:S(2)}) copy-start(f32[4,256,256]{1,2,0:T(8,128)} %copy.171) | copy-start | bytes 3145732
  607.1 4.0 copy-start.1
  (5 other events, 6.1 us)
Sparse Core Ops, SparseCore 0:
  101.1 32.1 all-gather.2
  142.1 31.6 reduce-scatter.2
  217.9 92.4 all-reduce.3
  312.4 32.4 all-gather.4
  353.8 31.6 reduce-scatter.4
where the time goes:
time: 623 us; the launch traced here: 618 us
  waiting for transfers between devices  254 us (41%)
  blocking collectives  159 us (26%)
  matrix products  66.3 us (11%)
  starting transfers between devices  51 us (8%)
  local copies, waits for them, and re-layouts  50.4 us (8%)
  other arithmetic  19.6 us (3%)
  between operations  17.9 us (3%)
    unnamed x6, waiting for transfers between devices  90.7 us
    all_gather x2, waiting for transfers between devices, mix_features(): lax.all_gather(lowered, 'ch', axis=1, tiled=True)  64.9 us
    psum x1, blocking collectives, shards(): norm_next = lax.psum(jnp.sum(residual_next * scaled), ('lat', 'ch'))  62.9 us
    psum x1, blocking collectives, shards(): norm_now = lax.psum(jnp.sum(residual * residual / precond), ('lat', 'ch'))  62.7 us
    reduce_scatter x2, waiting for transfers between devices, mix_features(): lax.psum_scatter(partial_terms.astype(jnp.bfloat16), 'ch', scatter_dimens...  62.4 us
    all_gather x1, blocking collectives, shards(): whole_field = lax.all_gather(summed, 'lat', axis=0, tiled=True)  27 us
    unnamed x57, local copies, waits for them, and re-layouts  20 us
    all_to_all x2, starting transfers between devices, spectral(): lax.all_to_all(real_part.astype(jnp.bfloat16), 'lat', split_axis=1, conca...  13.5 us
  transfers between devices with their start and end apart: 13, of which 11 were waited for; matrix products, arithmetic and copies ran while one was open for 6% of the time, Pallas kernels for 0%

commit v1 on v0

--- a/solution.py
+++ b/solution.py
@@ -115,20 +115,6 @@
     return jnp.dot(left, right, preferred_element_type=jnp.float32)
 
 
-def mix_features(rows, first, second, slope, flip):
-    lowered = rows.astype(jnp.bfloat16)
-    if flip:
-        part = first
-    else:
-        part = first
-    total = product(lax.all_gather(lowered, "ch", axis=1, tiled=True), part, flip)
-    hidden = (total * slope).astype(jnp.bfloat16)
-    partial_terms = product(hidden, second, flip)
-    return lax.psum_scatter(
-        partial_terms.astype(jnp.bfloat16), "ch", scatter_dimension=1, tiled=True
-    ).astype(jnp.float32)
-
-
 def shards(
     state,
     residual,
@@ -148,37 +134,32 @@
     bands, width, depth = direction.shape
     height = bands * lax.axis_size("lat")
     tabs = spectral_tables(width, height)
-    norm_now = lax.psum(jnp.sum(residual * residual / precond), ("lat", "ch"))
+    own_now = jnp.sum(residual * residual / precond)
+    own_square = jnp.sum(direction * direction)
 
-    def token_mix(rows, flip):
-        if flip:
-            return mix_features(rows, w_down, w_up, token_slope, flip)
-        return mix_features(rows, w_up, w_down, token_slope, flip)
+    slots = lax.broadcasted_iota(jnp.int32, obs_token.shape, 2)
+    live = jnp.where(slots < obs_count[:, :, None], obs_rinv, jnp.float32(0.0))
+    spread = jnp.zeros((height * width,), jnp.float32).at[obs_token.reshape(-1)].add(live.reshape(-1))
+    rsum = lax.psum_scatter(spread, "lat", scatter_dimension=0, tiled=True)
+
+    whole_weight = lax.all_gather(obs_weight, "ch", axis=0, tiled=True)
+    up = jnp.dot(w_down.astype(jnp.float32), whole_weight, precision=HIGH)
+    scaled_slope = (token_slope * up[None, :]).astype(jnp.bfloat16)
+    partial_q = product(scaled_slope, w_up, True)
+    q = lax.psum_scatter(partial_q.astype(jnp.bfloat16), "ch", scatter_dimension=1, tiled=True)
+    q = q.astype(jnp.float32) + obs_weight[None, :]
 
     first = direction + spectral(direction, spectral_slope, filter_in, filter_out, tabs, False)
     first_rows = first.reshape(bands * width, depth)
-    second_rows = first_rows + token_mix(first_rows, False)
-    projected = jnp.dot(second_rows, obs_weight, precision=HIGH)
-    summed = lax.psum(projected, "ch")
-    whole_field = lax.all_gather(summed, "lat", axis=0, tiled=True)
-    picked = whole_field[obs_token]
-    slots = lax.broadcasted_iota(jnp.int32, obs_token.shape, 2)
-    weighted = jnp.where(slots < obs_count[:, :, None], obs_rinv * picked, jnp.float32(0.0))
-    spread = (
-        jnp.zeros((height * width,), jnp.float32)
-        .at[obs_token.reshape(-1)]
-        .add(weighted.reshape(-1))
-    )
-    band_values = lax.psum_scatter(
-        spread.astype(jnp.bfloat16), "lat", scatter_dimension=0, tiled=True
-    ).astype(jnp.float32)
-    back_rows = band_values[:, None] * obs_weight[None, :]
-    back_mid_rows = back_rows + token_mix(back_rows, True)
-    back_mid = back_mid_rows.reshape(bands, width, depth)
+    projected = lax.psum(jnp.sum(first_rows * q, axis=1), "ch")
+    back_rows = rsum * projected
+    own_curve = own_square + jnp.sum(back_rows * projected) / lax.axis_size("ch")
+    sums = lax.psum(jnp.stack([own_now, own_curve]), ("lat", "ch"))
+    norm_now, curve = sums[0], sums[1]
+    back_mid = (back_rows[:, None] * q).reshape(bands, width, depth)
     image = (
         direction + back_mid + spectral(back_mid, spectral_slope, filter_out, filter_in, tabs, True)
     )
-    curve = lax.psum(jnp.sum(direction * image), ("lat", "ch"))
     alpha = norm_now / curve
     state_next = state + alpha * direction
     residual_next = residual - alpha * image

time: 623 us -> 448 us (0.72)
  waiting for transfers between devices: 254 us -> 91.4 us
  blocking collectives: 159 us -> 145 us
  matrix products: 66.3 us -> 60 us
    all_gather x2 -> x0, waiting for transfers between devices: 64.9 us -> none  [mix_features(): lax.all_gather(lowered, 'ch', axis=1, tiled=True)]
    reduce_scatter x2 -> x1, waiting for transfers between devices: 62.4 us -> 0.01 us  [shards(): lax.psum_scatter(partial_q.astype(jnp.bfloat16), 'ch', scatter_dimension=...]
    all_gather x1, blocking collectives: 27 us -> 9.42 us  [shards(): whole_weight = lax.all_gather(obs_weight, 'ch', axis=0, tiled=True)]
    unnamed x6 -> x3, waiting for transfers between devices: 90.7 us -> 77.1 us
    all_to_all x2, waiting for transfers between devices: 11.2 us -> 4.12 us  [spectral(): lax.all_to_all(real_part.astype(jnp.bfloat16), 'lat', split_axis=0, conca...]
    dot_general x2 -> x1, matrix products: 9.68 us -> 3.31 us  [shards(): up = jnp.dot(w_down.astype(jnp.float32), whole_weight, precision=HIGH)]
    unnamed x57 -> x69, local copies, waits for them, and re-layouts: 20 us -> 21.4 us
  transfers between devices with their start and end apart: 13 -> 10, of which waited for: 11 -> 7; matrix products, arithmetic and copies ran while one was open for 6% -> 18% of each run, Pallas kernels for 0% -> 0%
where the time goes in v1:
time: 448 us; the launch traced here: 440 us
  blocking collectives  145 us (32%)
  waiting for transfers between devices  91.4 us (20%)
  matrix products  60 us (13%)
  local copies, waits for them, and re-layouts  56.1 us (13%)
  starting transfers between devices  52.4 us (12%)
  between operations  20.7 us (5%)
  other arithmetic  15.1 us (3%)
    unnamed x3, waiting for transfers between devices  77.1 us
    psum x1, blocking collectives, shards(): sums = lax.psum(jnp.stack([own_now, own_curve]), ('lat', 'ch'))  66.7 us
    psum x1, blocking collectives, shards(): norm_next = lax.psum(jnp.sum(residual_next * scaled), ('lat', 'ch'))  62.6 us
    unnamed x69, local copies, waits for them, and re-layouts  21.4 us
    all_to_all x2, starting transfers between devices, spectral(): lax.all_to_all(real_part.astype(jnp.bfloat16), 'lat', split_axis=1, conca...  14.3 us
    all_to_all x2, starting transfers between devices, spectral(): lax.all_to_all(imag_part.astype(jnp.bfloat16), 'lat', split_axis=1, conca...  14.3 us
    all_to_all x2, starting transfers between devices, spectral(): lax.all_to_all(imag_part.astype(jnp.bfloat16), 'lat', split_axis=0, conca...  12 us
    all_to_all x2, starting transfers between devices, spectral(): lax.all_to_all(real_part.astype(jnp.bfloat16), 'lat', split_axis=0, conca...  11.6 us
  transfers between devices with their start and end apart: 10, of which 7 were waited for; matrix products, arithmetic and copies ran while one was open for 18% of the time, Pallas kernels for 0%

profile of v1, /device:TPU:1, one launch (start us, length us, event | category | flops | bytes accessed | tf_op | source)
XLA Modules:
  0.0 440.4 jit_solution(1341918259382670373)
XLA Ops:
  8.0 2.6 fusion.35
  11.5 8.6 %all-to-all-start = ((bf16[4,128,256]{2,0,1:T(4,128)(2,1)}), bf16[4,128,256]{2,0,1:T(4,128)(2,1)S(1)}, u32[]{:S(2)}, u32[]{:S(2)}) async-start(bf16[4,128,256]{2,0,1:T(4,128)(2,1)} %copy.111), calls=%async_computation | async-start | bytes 524288 | tf_op jit(solution)/shard_map/all_to_all | solution.py:73
  20.2 9.4 %all-gather = f32[4,1,256]{2,1,0:T(1,128)S(1)} all-gather(f32[1,1,256]{2,1,0:T(1,128)S(1)} %bitcast.333), channel_id=1, replica_groups=mesh['lat'=32,'ch'=4] {'ch'}, dimensions={0}, use_global_device_ids=true | all-gather | bytes 5120 | tf_op jit(solution)/shard_map/all_gather | solution.py:145
  29.6 3.3 fusion.305
  32.9 3.7 fusion.2
  40.0 9.5 %all-to-all-start.1 = ((bf16[4,128,256]{2,0,1:T(4,128)(2,1)}), bf16[4,128,256]{2,0,1:T(4,128)(2,1)}, u32[]{:S(2)}, u32[]{:S(2)}) async-start(bf16[4,128,256]{2,0,1:T(4,128)(2,1)} %copy.113), calls=%async_computation.1 | async-start | bytes 524288 | tf_op jit(solution)/shard_map/all_to_all | solution.py:76
  72.2 7.2 %all-to-all-start.2 = ((bf16[128,4,256]{2,1,0:T(4,128)(2,1)}), bf16[128,4,256]{2,1,0:T(4,128)(2,1)}, u32[]{:S(2)}, u32[]{:S(2)}) async-start(bf16[128,4,256]{2,1,0:T(4,128)(2,1)} %copy.129), calls=%async_computation.2 | async-start | bytes 524288 | tf_op jit(solution)/shard_map/all_to_all | solution.py:98
  84.2 4.1 all-to-all-done.2
  88.3 4.4 all-to-all-start.3
  92.8 3.9 scatter_custom_fusion
  107.3 3.1 fusion.8
  112.0 6.0 %psum.21 = f32[1024]{0:T(1024)S(1)} all-reduce(f32[1024]{0:T(1024)S(1)} %fusion.39), channel_id=1, replica_groups=mesh['lat'=32,'ch'=4] {'ch'}, use_global_device_ids=true, to_apply=%region_6.7 | all-reduce | flops 1024 | bytes 8192 | tf_op jit(solution)/shard_map/psum | solution.py:154
  118.0 77.0 %all-reduce.3.cloned.1.call-done = f32[32768]{0:T(1024)} async-done(((f32[32768]{0:T(1024)}), f32[32768]{0:T(1024)}) %all-reduce.3.cloned.1.call-update) | async-done | bytes 131088
  198.5 2.9 fusion.36
  203.2 5.7 %all-to-all-start.4 = ((bf16[4,128,256]{2,0,1:T(4,128)(2,1)}), bf16[4,128,256]{2,0,1:T(4,128)(2,1)}, u32[]{:S(2)}, u32[]{:S(2)}) async-start(bf16[4,128,256]{2,0,1:T(4,128)(2,1)} %copy.142), calls=%async_computation.5 | async-start | bytes 524288 | tf_op jit(solution)/shard_map/all_to_all | solution.py:73
  209.0 4.2 fusion.37
  214.9 3.0 all-to-all-done.4
  218.0 4.8 %all-to-all-start.5 = ((bf16[4,128,256]{2,0,1:T(4,128)(2,1)}), bf16[4,128,256]{2,0,1:T(4,128)(2,1)}, u32[]{:S(2)}, u32[]{:S(2)}) async-start(bf16[4,128,256]{2,0,1:T(4,128)(2,1)} %copy.145), calls=%async_computation.6 | async-start | bytes 524288 | tf_op jit(solution)/shard_map/all_to_all | solution.py:76
  222.8 2.5 fusion.41
  229.5 2.3 fusion.137
  248.7 7.7 %all-to-all-start.7 = ((bf16[128,4,256]{2,1,0:T(4,128)(2,1)}), bf16[128,4,256]{2,1,0:T(4,128)(2,1)S(1)}, u32[]{:S(2)}, u32[]{:S(2)}) async-start(bf16[128,4,256]{2,1,0:T(4,128)(2,1)} %copy.166), calls=%async_computation.8 | async-start | bytes 524288 | tf_op jit(solution)/shard_map/all_to_all | solution.py:101
  259.3 5.9 %all-to-all-done.7 = bf16[128,4,256]{2,1,0:T(4,128)(2,1)S(1)} async-done(((bf16[128,4,256]{2,1,0:T(4,128)(2,1)}), bf16[128,4,256]{2,1,0:T(4,128)(2,1)S(1)}, u32[]{:S(2)}, u32[]{:S(2)}) %all-to-all-start.7) | async-done | bytes 262176 | tf_op jit(solution)/shard_map/all_to_all | solution.py:101
  265.2 4.4 all-to-all-start.6
  271.8 2.5 copy.169
  274.3 2.6 copy.170
  278.8 2.5 copy.138
  281.3 66.7 %psum.22 = f32[2]{0:T(128)S(1)} all-reduce(f32[2]{0:T(128)S(1)} %pad_maximum_fusion), channel_id=1, replica_groups=mesh['lat'=32,'ch'=4] {'lat','ch'}, use_global_device_ids=true, to_apply=%region_8.9 | all-reduce | flops 2 | bytes 16 | tf_op jit(solution)/shard_map/psum | solution.py:157
  354.4 4.8 %multiply_reduce_fusion = (f32[]{:T(128)}, f32[4,256,256]{1,2,0:T(8,128)}, f32[4,256,256]{1,2,0:T(8,128)}) fusion(f32[4,256,256]{1,2,0:T(8,128)} %copy.170, f32[4,256,256]{1,2,0:T(8,128)S(1)} %copy-done.13, f32[4,256,256]{2,1,0:T(8,128)S(1)} %fusion.63, bf16[4,128,256]{2,0,1:T(4,128)(2,1)S(1)} %bitcast.322, f32[4,256,256]{1,2,0:T(8,128)S(1)} %copy-done.4, ...), kind=kOutput, calls=%fused_computation.66 | convolution fusion | flops 405209088 | bytes 7602184 | tf_op jit(solution)/shard_map/kw,lkd->lwd/dot_general | solution.py:34
  359.3 62.6 %psum.23 = f32[]{:T(128)} all-reduce(f32[]{:T(128)} %get-tuple-element.12), channel_id=1, replica_groups=mesh['lat'=32,'ch'=4] {'lat','ch'}, use_global_device_ids=true, to_apply=%region_10.11 | all-reduce | flops 1 | bytes 8 | tf_op jit(solution)/shard_map/psum | solution.py:167
  423.2 3.1 multiply_add_fusion
  426.3 2.6 copy.172
  428.9 2.5 copy.174
  (149 shorter events, 83.5 us)
Async XLA Ops:
  8.0 24.9 %copy-start = (bf16[1024,1024]{1,0:T(8,128)(2,1)S(1)}, bf16[1024,1024]{1,0:T(8,128)(2,1)}, u32[]{:S(2)}) copy-start(bf16[1024,1024]{1,0:T(8,128)(2,1)} %param.22) | copy-start | bytes 6291460
  8.0 12.1 %copy-start.23 = (f32[256]{0:T(256)S(1)}, f32[256]{0:T(256)}, u32[]{:S(2)}) copy-start(f32[256]{0:T(256)} %param.24) | copy-start | bytes 3076
  11.5 28.4 %all-to-all-start = ((bf16[4,128,256]{2,0,1:T(4,128)(2,1)}), bf16[4,128,256]{2,0,1:T(4,128)(2,1)S(1)}, u32[]{:S(2)}, u32[]{:S(2)}) async-start(bf16[4,128,256]{2,0,1:T(4,128)(2,1)} %copy.111), calls=%async_computation | async-start | bytes 524288 | tf_op jit(solution)/shard_map/all_to_all | solution.py:73
  20.1 90.3 %reduce-scatter.2.cloned.1.call-start = ((), (), s32[]{:S(2)}) async-start(), calls=%async_computation.9 | async-start | bytes 2621440 | tf_op jit(solution)/shard_map/reduce_scatter | solution.py:149
  20.1 12.8 %copy-start.27 = (bf16[1024,1024]{1,0:T(8,128)(2,1)S(1)}, bf16[1024,1024]{1,0:T(8,128)(2,1)}, u32[]{:S(2)}) copy-start(bf16[1024,1024]{1,0:T(8,128)(2,1)} %param.18) | copy-start | bytes 6291460
  37.8 13.6 %copy-start.24 = (f32[1,4,128]{2,1,0:T(4,128)S(1)}, f32[1,4,128]{2,1,0:T(4,128)}, u32[]{:S(2)}) copy-start(f32[1,4,128]{2,1,0:T(4,128)} %param.27) | copy-start | bytes 6148
  37.8 13.6 %copy-start.26 = (s32[1,4]{1,0:T(1,128)S(1)}, s32[1,4]{1,0:T(1,128)}, u32[]{:S(2)}) copy-start(s32[1,4]{1,0:T(1,128)} %param.26) | copy-start | bytes 52
  40.0 11.6 %copy-start.21 = (bf16[4,128,256]{2,0,1:T(4,128)(2,1)}, bf16[4,128,256]{2,0,1:T(4,128)(2,1)S(1)}, u32[]{:S(2)}) copy-start(bf16[4,128,256]{2,0,1:T(4,128)(2,1)S(1)} %all-to-all-done) | copy-start | bytes 786436
  40.0 18.4 %all-to-all-start.1 = ((bf16[4,128,256]{2,0,1:T(4,128)(2,1)}), bf16[4,128,256]{2,0,1:T(4,128)(2,1)}, u32[]{:S(2)}, u32[]{:S(2)}) async-start(bf16[4,128,256]{2,0,1:T(4,128)(2,1)} %copy.113), calls=%async_computation.1 | async-start | bytes 524288 | tf_op jit(solution)/shard_map/all_to_all | solution.py:76
  60.1 3.2 copy-start.19
  60.1 3.8 copy-start.18
  60.1 4.4 copy-start.12
  63.3 2.4 copy-start.7
  72.2 20.5 %copy-start.25 = (s32[1,4,128]{2,1,0:T(4,128)S(1)}, s32[1,4,128]{2,1,0:T(4,128)}, u32[]{:S(2)}) copy-start(s32[1,4,128]{2,1,0:T(4,128)} %param.25) | copy-start | bytes 6148
  72.2 24.4 %copy-start.28 = (u32[128]{0:T(128)S(1)}, u32[128]{0:T(128)}, u32[]{:S(2)}) copy-start(u32[128]{0:T(128)} %constant.68) | copy-start | bytes 1540
  72.2 16.1 %all-to-all-start.2 = ((bf16[128,4,256]{2,1,0:T(4,128)(2,1)}), bf16[128,4,256]{2,1,0:T(4,128)(2,1)}, u32[]{:S(2)}, u32[]{:S(2)}) async-start(bf16[128,4,256]{2,1,0:T(4,128)(2,1)} %copy.129), calls=%async_computation.2 | async-start | bytes 524288 | tf_op jit(solution)/shard_map/all_to_all | solution.py:98
  88.3 13.5 %all-to-all-start.3 = ((bf16[128,4,256]{2,1,0:T(4,128)(2,1)}), bf16[128,4,256]{2,1,0:T(4,128)(2,1)}, u32[]{:S(2)}, u32[]{:S(2)}) async-start(bf16[128,4,256]{2,1,0:T(4,128)(2,1)} %copy.134), calls=%async_computation.3 | async-start | bytes 524288 | tf_op jit(solution)/shard_map/all_to_all | solution.py:101
  92.7 102.3 %all-reduce.3.cloned.1.call-start = ((), (), s32[]{:S(2)}) async-start(), calls=%async_computation.10 | async-start | bytes 262144
  203.2 14.8 %all-to-all-start.4 = ((bf16[4,128,256]{2,0,1:T(4,128)(2,1)}), bf16[4,128,256]{2,0,1:T(4,128)(2,1)}, u32[]{:S(2)}, u32[]{:S(2)}) async-start(bf16[4,128,256]{2,0,1:T(4,128)(2,1)} %copy.142), calls=%async_computation.5 | async-start | bytes 524288 | tf_op jit(solution)/shard_map/all_to_all | solution.py:73
  208.9 16.3 %slice-start = ((f32[2,2,128,128]{3,2,1,0:T(8,128)}), f32[1,2,128,128]{3,2,1,0:T(8,128)S(1)}, s32[]{:S(2)}) async-start(f32[2,2,128,128]{3,2,1,0:T(8,128)} %param.21), calls=%async_computation.11 | async-start | bytes 262144 | tf_op jit(solution)/shard_map/slice | solution.py:56
  218.0 13.9 %all-to-all-start.5 = ((bf16[4,128,256]{2,0,1:T(4,128)(2,1)}), bf16[4,128,256]{2,0,1:T(4,128)(2,1)}, u32[]{:S(2)}, u32[]{:S(2)}) async-start(bf16[4,128,256]{2,0,1:T(4,128)(2,1)} %copy.145), calls=%async_computation.6 | async-start | bytes 524288 | tf_op jit(solution)/shard_map/all_to_all | solution.py:76
  231.9 7.5 %copy-start.20 = (f32[1,2,128,128]{2,3,1,0:T(8,128)S(1)}, f32[1,2,128,128]{2,3,1,0:T(8,128)}, u32[]{:S(2)}) copy-start(f32[1,2,128,128]{2,3,1,0:T(8,128)} %copy.209) | copy-start | bytes 393220
  235.4 3.3 copy-start.16
  235.4 4.6 %copy-start.17 = (bf16[128,4,256]{2,0,1:T(8,128)(2,1)S(1)}, bf16[128,4,256]{2,0,1:T(8,128)(2,1)}, u32[]{:S(2)}) copy-start(bf16[128,4,256]{2,0,1:T(8,128)(2,1)} %all_to_all.123) | copy-start | bytes 786436
  243.7 3.2 copy-start.10
  248.7 16.5 %all-to-all-start.7 = ((bf16[128,4,256]{2,1,0:T(4,128)(2,1)}), bf16[128,4,256]{2,1,0:T(4,128)(2,1)S(1)}, u32[]{:S(2)}, u32[]{:S(2)}) async-start(bf16[128,4,256]{2,1,0:T(4,128)(2,1)} %copy.166), calls=%async_computation.8 | async-start | bytes 524288 | tf_op jit(solution)/shard_map/all_to_all | solution.py:101
  265.2 9.1 %copy-start.22 = (bf16[128,4,256]{2,1,0:T(4,128)(2,1)}, bf16[128,4,256]{2,1,0:T(4,128)(2,1)S(1)}, u32[]{:S(2)}) copy-start(bf16[128,4,256]{2,1,0:T(4,128)(2,1)S(1)} %all-to-all-done.7) | copy-start | bytes 786436
  265.2 86.9 %all-to-all-start.6 = ((bf16[128,4,256]{2,1,0:T(4,128)(2,1)}), bf16[128,4,256]{2,1,0:T(4,128)(2,1)}, u32[]{:S(2)}, u32[]{:S(2)}) async-start(bf16[128,4,256]{2,1,0:T(4,128)(2,1)} %copy.161), calls=%async_computation.7 | async-start | bytes 524288 | tf_op jit(solution)/shard_map/all_to_all | solution.py:98
  274.3 73.6 %copy-start.3 = (f32[1024,256]{1,0:T(8,128)S(1)}, f32[1024,256]{1,0:T(8,128)}, u32[]{:S(2)}) copy-start(f32[1024,256]{1,0:T(8,128)} %copy-done.2) | copy-start | bytes 3145732
  349.3 5.1 %copy-start.4 = (f32[4,256,256]{1,2,0:T(8,128)S(1)}, f32[4,256,256]{1,2,0:T(8,128)}, u32[]{:S(2)}) copy-start(f32[4,256,256]{1,2,0:T(8,128)} %copy.137) | copy-start | bytes 3145732
  352.2 2.3 copy-start.13
  426.3 5.2 %copy-start.14 = (f32[4,256,256]{1,2,0:T(8,128)S(1)}, f32[4,256,256]{1,2,0:T(8,128)}, u32[]{:S(2)}) copy-start(f32[4,256,256]{1,2,0:T(8,128)} %get-tuple-element.22) | copy-start | bytes 3145732
  (8 other events, 13.5 us)
Sparse Core Ops, SparseCore 0:
  36.8 30.4 reduce-scatter.1
Sparse Core Ops, SparseCore 1:
  96.7 98.2 all-reduce.2

commit v2 on v1

v2 whole, which is shorter than its diff:
```python
import functools
import math

import jax
import jax.numpy as jnp
import ml_dtypes
import numpy as np
from jax import lax
from jax.experimental import pallas as pl
from jax.experimental.pallas import tpu as pltpu
from jax.sharding import PartitionSpec as P

MESH = pl.DeviceIdType.MESH
F32 = jnp.float32
BF = jnp.bfloat16
NT = (((1,), (1,)), ((), ()))
N_LAT = 32
N_CH = 4


def halves(table):
    high = table.astype(ml_dtypes.bfloat16)
    low = (table - high.astype(np.float32)).astype(ml_dtypes.bfloat16)
    return high, low


def angles(length, count):
    place = (np.arange(count)[:, None] * np.arange(length)[None, :]) % length
    angle = (2.0 * math.pi / length) * place.astype(np.float64)
    return np.cos(angle).astype(np.float32), np.sin(angle).astype(np.float32)


def make_tables(width, height):
    count = width // 2
    cos, sin = angles(width, count)
    scale = np.where(np.arange(count) == 0, 1.0, 2.0).astype(np.float32)[:, None] / width
    per = count // N_LAT

    def spectral_rows(c, s):
        both = np.stack([c.reshape(N_LAT, per, width), -s.reshape(N_LAT, per, width)], axis=1)
        return both.reshape(2 * count, width).astype(np.float32)

    plain = spectral_rows(cos, sin)
    inverse = spectral_rows(cos * scale, sin * scale)
    lat_cos, lat_sin = angles(height, height)
    mix = np.zeros((2, height, height, 2), np.float32)
    mix[0, :, :, 0] = lat_cos
    mix[0, :, :, 1] = lat_sin
    mix[1, :, :, 0] = -lat_sin
    mix[1, :, :, 1] = lat_cos
    mix = mix.reshape(2 * height, 2 * height)
    unmix = np.ascontiguousarray(mix.T) / np.float32(height)

    def left(table, parts):
        high, low = halves(np.ascontiguousarray(table))
        return np.concatenate([high, low, high][:parts], axis=1)

    return dict(
        lon=left(plain, 3),
        back=left(inverse.T, 2),
        lon_adj=inverse,
        back_adj=left(plain.T, 2),
        mix=left(mix, 2),
        unmix=left(unmix, 3),
    )


def split(x):
    high = x.astype(BF)
    return high, (x - high.astype(F32)).astype(BF)


def dot(a, b):
    return jnp.dot(a, b, preferred_element_type=F32)


def dot_nt(a, b):
    return lax.dot_general(a, b, NT, preferred_element_type=F32)


def right3(x):
    high, low = split(x)
    return jnp.concatenate([high, high, low], axis=0)


def left3(x):
    high, low = split(x)
    return jnp.concatenate([high, low, high], axis=1)


def kernel(
    count_ref, d_hbm, r_hbm, p_hbm, slope_hbm, sslope_hbm, fin_hbm, fout_hbm, wup_hbm, wdown_hbm,
    ow_hbm, tok_hbm, rinv_hbm, lon_hbm, back_hbm, lona_hbm, backa_hbm, mix_hbm, unmix_hbm,
    rn_hbm, scal_ref,
    d, r, p, slope, sslope, fin, fout, wup, wdown, tok, rinv, lon_t, back_t, lona_t, backa_t,
    mix_t, unmix_t, owz, sl, wk, wl, wupu, g_far, g_own, g_next, g_prev, q, qcat, esum, base,
    spread, lat_rows, send, recv, rpart, rrecv, out_far, out_next, out_prev, out_acc,
    in_far, in_next, in_prev, in_acc, proj, ar1, ar1z, ar2, ar2z, rn,
    load_sem, a_send, a_recv, z_send, z_recv, s_send, s_recv, out_sem,
):
    me = lax.axis_index("lat")
    z = lax.axis_index("ch")
    px, py, pc = me // 8, (me // 2) % 4, me % 2
    z_next, z_prev, z_far = (z + 1) % 4, (z + 3) % 4, (z + 2) % 4

    def peer(o):
        dx, dy, dc = o // 8, (o // 2) % 4, o % 2
        return ((px + dx) % 4) * 8 + ((py + dy) % 4) * 2 + (pc + dc) % 2

    loads = [
        pltpu.make_async_copy(src, dst, load_sem.at[i])
        for i, (src, dst) in enumerate([
            (d_hbm, d), (lon_hbm, lon_t), (tok_hbm, tok), (rinv_hbm, rinv), (ow_hbm, owz.at[z]),
            (wdown_hbm, wdown), (wup_hbm, wup), (slope_hbm, slope), (mix_hbm, mix_t), (fin_hbm, fin),
            (fout_hbm, fout), (sslope_hbm, sslope), (unmix_hbm, unmix_t), (back_hbm, back_t),
            (r_hbm, r), (p_hbm, p), (lona_hbm, lona_t), (backa_hbm, backa_t),
        ])
    ]
    for copy in loads:
        copy.start()
    (l_d, l_lon, l_tok, l_rinv, l_ow, l_wdown, l_wup, l_slope, l_mix, l_fin, l_fout, l_sslope,
     l_unmix, l_back, l_r, l_p, l_lona, l_backa) = loads

    barrier = pltpu.get_barrier_semaphore()

    def greet(o, carry):
        pl.semaphore_signal(barrier, inc=1, device_id=(peer(o), z), device_id_type=MESH)
        return carry

    lax.fori_loop(1, N_LAT, greet, 0)
    for other in (z_next, z_prev, z_far):
        pl.semaphore_signal(barrier, inc=1, device_id=(me, other), device_id_type=MESH)

    def to_all(src_of, dst, send_sem, recv_sem):
        def go(o, carry):
            other = peer(o)
            pltpu.make_async_remote_copy(
                src_of(other), dst, send_sem, recv_sem, device_id=(other, z), device_id_type=MESH
            ).start()
            return carry

        lax.fori_loop(1, N_LAT, go, 0)

    def wait_for(ref, n, sem):
        part = ref.at[pl.ds(0, n)]
        pltpu.make_async_copy(part, part, sem).wait()

    def scatter(stage, c):
        i = stage * 2 + c
        recv[i, me] = send[i, me]
        to_all(lambda o: send.at[i, o], recv.at[i, me], a_send.at[i], a_recv.at[i])

    def arrive(stage, c):
        i = stage * 2 + c
        wait_for(recv.at[i], N_LAT - 1, a_recv.at[i])
        return recv[i]

    def z_copy(src, dst, other, k):
        copy = pltpu.make_async_remote_copy(
            src, dst, z_send.at[k], z_recv.at[k], device_id=(me, other), device_id_type=MESH
        )
        copy.start()
        return copy

    def pack_rows(stage, c, out):
        rows = out.reshape(N_LAT, 8, 512)
        rows = jnp.concatenate([rows[:, :, 128 * h:128 * h + 128] for h in range(4)], axis=1)
        send[stage * 2 + c] = rows.astype(BF)

    l_d.wait()
    l_lon.wait()
    for c in range(2):
        x = jnp.concatenate([d[h, :, 128 * c:128 * c + 128] for h in range(4)], axis=1)
        pack_rows(0, c, dot(lon_t[...], right3(x)))

    l_tok.wait()
    l_rinv.wait()
    where_high, where_low = [], []
    rows_high = lax.broadcasted_iota(jnp.int32, (256, 128), 0)
    rows_low = lax.broadcasted_iota(jnp.int32, (128, 128), 0)
    lane = lax.broadcasted_iota(jnp.int32, (1, 128), 1)
    for j in range(4):
        token = tok[0, j:j + 1, :]
        live = jnp.where(lane < count_ref[0, j], rinv[0, j:j + 1, :], 0.0)
        hot = jnp.where(rows_high == (token >> 7), 1.0, 0.0).astype(BF)
        value = jnp.where(rows_low == (token & 127), live, 0.0)
        v0, rest = value.astype(BF), value - value.astype(BF).astype(F32)
        v1, v2 = split(rest)
        where_high += [hot, hot, hot]
        where_low += [v0, v1, v2]
    spread_now = dot_nt(jnp.concatenate(where_high, axis=1), jnp.concatenate(where_low, axis=1))
    rpart[...] = spread_now.reshape(N_LAT, 8, 128)

    l_ow.wait()
    pl.semaphore_wait(barrier, N_LAT - 1 + N_CH - 1)

    ow_copies = [
        pltpu.make_async_remote_copy(
            owz.at[z], owz.at[z], s_send.at[0], s_recv.at[0], device_id=(me, other),
            device_id_type=MESH)
        for other in (z_next, z_prev, z_far)
    ]
    for copy in ow_copies:
        copy.start()
    scatter(0, 0)
    scatter(0, 1)
    rrecv[me] = rpart[me]
    to_all(lambda o: rpart.at[o], rrecv.at[me], s_send.at[1], s_recv.at[1])

    l_wdown.wait()
    l_wup.wait()
    l_slope.wait()
    wait_for(owz, 3, s_recv.at[0])
    weight = jnp.concatenate([owz[j] for j in range(4)], axis=1)
    w0, rest = weight.astype(BF), weight - weight.astype(BF).astype(F32)
    w1, w2 = split(rest)
    sub = lax.broadcasted_iota(jnp.int32, (8, 1024), 0)
    zero = jnp.zeros((8, 1024), F32)
    parts = jnp.where(sub == 0, w0.astype(F32), jnp.where(sub == 1, w1.astype(F32), jnp.where(
        sub == 2, w2.astype(F32), zero)))
    u = jnp.sum(dot_nt(parts.astype(BF), wdown[...]), axis=0, keepdims=True)
    wupu[...] = (wup[...].astype(F32) * u).astype(BF)

    def share(owner, dst):
        cols = wupu[pl.ds(pl.multiple_of(owner * 256, 256), 256), :]

        def rows(i, carry):
            at = pl.ds(pl.multiple_of(i * 256, 256), 256)
            dst[at, :] = dot_nt(slope[at, :], cols).astype(dst.dtype)
            return carry

        lax.fori_loop(0, 4, rows, 0)

    top, low = pl.ds(0, 512), pl.ds(512, 512)
    share(z_far, out_far)
    z_copies = [
        z_copy(out_far.at[top], in_far.at[top], z_next, 0),
        z_copy(out_far.at[low], in_far.at[low], z_prev, 1),
    ]
    share(z_next, g_next)
    out_next[...] = g_next[low, :].astype(BF)
    z_copies.append(z_copy(out_next, in_next, z_next, 2))
    share(z_prev, g_prev)
    out_prev[...] = g_prev[top, :].astype(BF)
    z_copies.append(z_copy(out_prev, in_prev, z_prev, 3))
    share(z, g_own)

    l_fin.wait()
    l_fout.wait()
    for f, filt in enumerate((fin, fout)):
        for c in range(2):
            real, imag = filt[0, c], filt[1, c]
            whole = jnp.concatenate([
                jnp.concatenate([real, imag], axis=1), jnp.concatenate([-imag, real], axis=1)
            ], axis=0)
            high, low_part = split(whole)
            wk[f * 2 + c] = jnp.concatenate([high, high, low_part], axis=0)
            wl[f * 2 + c] = jnp.concatenate([high, high, low_part], axis=1)
    l_sslope.wait()
    for part in range(2):
        for c in range(2):
            spread[pl.ds(0, 512), :] = sslope[part, :, 128 * c:128 * c + 128].astype(F32)
            for kk in range(4):
                sl[c, 128 * kk:128 * kk + 128, 128 * part:128 * part + 128] = (
                    spread[pl.ds(kk, 128, stride=4), :]
                )
    l_mix.wait()
    l_unmix.wait()

    def middle(stage, c, adjoint):
        spread[...] = arrive(stage, c).reshape(1024, 128).astype(F32)
        x = jnp.concatenate([spread[pl.ds(kk, 256, stride=4), :] for kk in range(4)], axis=1)
        x = x.astype(BF)
        m = dot(mix_t[...], jnp.concatenate([x, x], axis=0))
        m = jnp.concatenate([
            jnp.concatenate([m[0:128, 128 * kk:128 * kk + 128], m[128:256, 128 * kk:128 * kk + 128]], axis=1)
            for kk in range(4)
        ], axis=0)
        if adjoint:
            m = dot_nt(left3(m), wl[2 + c])
            m = dot_nt(left3(m * sl[c]), wl[c])
        else:
            m = dot(left3(m), wk[c])
            m = dot(left3(m * sl[c]), wk[2 + c])
        m = jnp.concatenate([
            jnp.concatenate([m[128 * kk:128 * kk + 128, 128 * part:128 * part + 128] for kk in range(4)], axis=1)
            for part in range(2)
        ], axis=0)
        m = dot(unmix_t[...], right3(m))
        for kk in range(4):
            spread[pl.ds(kk, 256, stride=4), :] = m[:, 128 * kk:128 * kk + 128]
        send[stage * 2 + 2 + c] = spread[...].astype(BF).reshape(N_LAT, 32, 128)
        scatter(stage + 1, c)

    def back(stage, c, table):
        rows = arrive(stage, c).astype(F32)
        x = jnp.concatenate([rows[:, 8 * h:8 * h + 8, :].reshape(256, 128) for h in range(4)], axis=1)
        x = x.astype(BF)
        return dot(table[...], jnp.concatenate([x, x], axis=0))

    middle(0, 0, False)
    middle(0, 1, False)

    z_copies[0].wait_recv()
    z_copies[1].wait_recv()
    out_acc[top, :] = (g_next[top, :] + in_far[top, :].astype(F32)).astype(BF)
    acc_next = z_copy(out_acc.at[top], in_acc.at[top], z_next, 4)
    out_acc[low, :] = (g_prev[low, :] + in_far[low, :].astype(F32)).astype(BF)
    acc_prev = z_copy(out_acc.at[low], in_acc.at[low], z_prev, 5)
    z_copies += [acc_next, acc_prev]

    wait_for(rrecv, N_LAT - 1, s_recv.at[1])
    rsum = jnp.sum(rrecv[...], axis=0)
    rrow = jnp.concatenate([rsum[i:i + 1, :] for i in range(8)], axis=1)

    l_r.wait()
    l_p.wait()
    l_back.wait()
    own_now = jnp.sum(r[...] * r[...] / p[...], keepdims=True)[0]
    own_square = jnp.sum(d[...] * d[...], keepdims=True)[0]

    z_copies[2].wait_recv()
    z_copies[3].wait_recv()
    acc_next.wait_recv()
    acc_prev.wait_recv()
    own_weight = owz[z]
    q_top = g_own[top, :] + in_acc[top, :].astype(F32) + in_prev[...].astype(F32) + own_weight
    q_low = g_own[low, :] + in_acc[low, :].astype(F32) + in_next[...].astype(F32) + own_weight
    q[top, :] = q_top
    q[low, :] = q_low
    for h in range(4):
        high, low_part = split(q[256 * h:256 * h + 256, :])
        qcat[h] = jnp.concatenate([high, high, low_part], axis=0)

    for c in range(2):
        f = back(1, c, back_t)
        at = pl.ds(128 * c, 128)
        for h in range(4):
            rows = pl.ds(256 * h, 256)
            e = (d[h, :, at] + f[:, 128 * h:128 * h + 128]) * q[rows, at]
            if c == 0:
                esum[rows, :] = e
            else:
                esum[rows, :] = esum[rows, :] + e
    ehigh, elow = split(esum[...])
    mine = dot_nt(jnp.ones((8, 256), BF), jnp.concatenate([ehigh, elow], axis=1))
    proj[z] = mine[0:1, :]
    p_copies = [
        pltpu.make_async_remote_copy(
            proj.at[z], proj.at[z], s_send.at[2], s_recv.at[2], device_id=(me, other),
            device_id_type=MESH)
        for other in (z_next, z_prev, z_far)
    ]
    for copy in p_copies:
        copy.start()
    l_lona.wait()
    l_backa.wait()
    wait_for(proj, 3, s_recv.at[2])
    projected = (proj[0] + proj[1]) + (proj[2] + proj[3])
    gain = rrow * projected

    outs = []
    for h in range(4):
        outs.append(dot(left3(lona_t[...] * gain[:, 256 * h:256 * h + 256]), qcat[h]))
    for c in range(2):
        pack_rows(2, c, jnp.concatenate([o[:, 128 * c:128 * c + 128] for o in outs], axis=1))
        scatter(2, c)

    curve = own_square + jnp.sum(gain * projected, keepdims=True) * 0.25
    ar1[me] = jnp.where(lane == 0, own_now, jnp.where(lane == 1, curve, 0.0))
    to_all(lambda o: ar1.at[me], ar1.at[me], s_send.at[3], s_recv.at[3])

    column = jnp.transpose(jnp.broadcast_to(gain, (8, 1024)))[:, 0:1]
    for h in range(4):
        base[h] = d[h] + column[256 * h:256 * h + 256, :] * q[256 * h:256 * h + 256, :]

    wait_for(ar1, N_LAT - 1, s_recv.at[3])
    ar1z[z] = jnp.sum(ar1[...], axis=0)
    one_copies = [
        pltpu.make_async_remote_copy(
            ar1z.at[z], ar1z.at[z], s_send.at[4], s_recv.at[4], device_id=(me, other),
            device_id_type=MESH)
        for other in (z_next, z_prev, z_far)
    ]
    for copy in one_copies:
        copy.start()

    middle(2, 0, True)
    middle(2, 1, True)

    wait_for(ar1z, 3, s_recv.at[4])
    sums = (ar1z[0] + ar1z[1]) + (ar1z[2] + ar1z[3])
    norm_now, all_curve = sums[:, 0:1], sums[:, 1:2]
    alpha = norm_now / all_curve

    total = jnp.zeros((1, 1), F32)
    for c in range(2):
        f = back(3, c, backa_t)
        at = pl.ds(128 * c, 128)
        for h in range(4):
            image = base[h, :, at] + f[:, 128 * h:128 * h + 128]
            after = r[h, :, at] - alpha * image
            rn[h, :, at] = after
            total = total + jnp.sum(after * after / p[h, :, at], keepdims=True)
    out_copy = pltpu.make_async_copy(rn, rn_hbm, out_sem)
    out_copy.start()
    ar2[me] = jnp.where(lane == 0, total, 0.0)
    to_all(lambda o: ar2.at[me], ar2.at[me], s_send.at[5], s_recv.at[5])
    wait_for(ar2, N_LAT - 1, s_recv.at[5])
    ar2z[z] = jnp.sum(ar2[...], axis=0)
    two_copies = [
        pltpu.make_async_remote_copy(
            ar2z.at[z], ar2z.at[z], s_send.at[6], s_recv.at[6], device_id=(me, other),
            device_id_type=MESH)
        for other in (z_next, z_prev, z_far)
    ]
    for copy in two_copies:
        copy.start()
    wait_for(ar2z, 3, s_recv.at[6])
    norm_next = ((ar2z[0] + ar2z[1]) + (ar2z[2] + ar2z[3]))[:, 0:1]
    beta = norm_next / norm_now
    scal_ref[...] = jnp.where(lane == 0, alpha, jnp.where(lane == 1, beta, 0.0))

    for i in range(8):
        wait_for(send.at[i], N_LAT - 1, a_send.at[i])
    for copy in z_copies:
        copy.wait_send()
    wait_for(owz, 3, s_send.at[0])
    wait_for(rpart, N_LAT - 1, s_send.at[1])
    wait_for(proj, 3, s_send.at[2])
    wait_for(ar1, N_LAT - 1, s_send.at[3])
    wait_for(ar1z, 3, s_send.at[4])
    wait_for(ar2, N_LAT - 1, s_send.at[5])
    wait_for(ar2z, 3, s_send.at[6])
    out_copy.wait()


def finish(scal, state, direction, rn, precond, state_out, rn_out, direction_out):
    alpha, beta = scal[0, 0], scal[0, 1]
    now = direction[...]
    after = rn[...]
    state_out[...] = state[...] + alpha * now
    rn_out[...] = after
    direction_out[...] = after / precond[...] + beta * now


def shards(
    state, residual, direction, precond, token_slope, spectral_slope, filter_in, filter_out,
    w_up, w_down, obs_weight, obs_token, obs_count, obs_rinv,
):
    bands, width, depth = direction.shape
    tabs = make_tables(width, bands * N_LAT)
    tables = [jnp.asarray(tabs[k]) for k in ("lon", "back", "lon_adj", "back_adj", "mix", "unmix")]
    hbm = pl.BlockSpec(memory_space=pl.ANY)
    vm = pltpu.VMEM
    field = vm((4, 256, 256), F32)
    scratch = [
        field, field, field, vm((1024, 1024), BF), vm((2, 512, 256), BF),
        vm((2, 2, 128, 128), F32), vm((2, 2, 128, 128), F32), vm((1024, 1024), BF),
        vm((1024, 1024), BF), vm((1, 4, 128), jnp.int32), vm((1, 4, 128), F32),
        vm((256, 768), BF), vm((256, 512), BF), vm((256, 256), F32), vm((256, 512), BF),
        vm((256, 512), BF), vm((256, 768), BF),
        vm((4, 1, 256), F32), vm((2, 512, 256), F32), vm((4, 768, 256), BF), vm((4, 256, 768), BF),
        vm((1024, 1024), BF), vm((8, 128), F32), vm((1024, 256), F32), vm((1024, 256), F32),
        vm((1024, 256), F32), vm((1024, 256), F32), vm((4, 768, 256), BF), vm((1024, 128), F32),
        field, vm((1024, 128), F32), vm((8, 128), F32),
        vm((8, N_LAT, 32, 128), BF), vm((8, N_LAT, 32, 128), BF),
        vm((N_LAT, 8, 128), F32), vm((N_LAT, 8, 128), F32),
        vm((1024, 256), BF), vm((512, 256), BF), vm((512, 256), BF), vm((1024, 256), BF),
        vm((1024, 256), BF), vm((512, 256), BF), vm((512, 256), BF), vm((1024, 256), BF),
        vm((4, 1, 1024), F32), vm((N_LAT, 1, 128), F32), vm((4, 1, 128), F32),
        vm((N_LAT, 1, 128), F32), vm((4, 1, 128), F32), field,
        pltpu.SemaphoreType.DMA((18,)), pltpu.SemaphoreType.DMA((8,)), pltpu.SemaphoreType.DMA((8,)),
        pltpu.SemaphoreType.DMA((6,)), pltpu.SemaphoreType.DMA((6,)), pltpu.SemaphoreType.DMA((7,)),
        pltpu.SemaphoreType.DMA((7,)), pltpu.SemaphoreType.DMA,
    ]
    rn, scal = pl.pallas_call(
        kernel,
        out_shape=(
            jax.ShapeDtypeStruct((4, 256, 256), F32), jax.ShapeDtypeStruct((1, 128), F32),
        ),
        in_specs=[pl.BlockSpec(memory_space=pltpu.SMEM)] + [hbm] * 18,
        out_specs=(hbm, pl.BlockSpec(memory_space=pltpu.VMEM)),
        scratch_shapes=scratch,
        compiler_params=pltpu.CompilerParams(
            collective_id=0, has_side_effects=True, vmem_limit_bytes=56 << 20
        ),
        cost_estimate=pl.CostEstimate(flops=4 * 10**9, bytes_accessed=14 << 20, transcendentals=0),
        name="spectral_step",
    )(
        obs_count, direction, residual, precond, token_slope,
        spectral_slope.reshape(2, 512, 256), filter_in, filter_out, w_up, w_down,
        obs_weight.reshape(1, 256), obs_token, obs_rinv, *tables,
    )
    block = pl.BlockSpec((1, 256, 256), lambda i: (i, 0, 0))
    shape = jax.ShapeDtypeStruct((4, 256, 256), F32)
    return pl.pallas_call(
        finish,
        out_shape=(shape, shape, shape),
        grid=(4,),
        in_specs=[pl.BlockSpec(memory_space=pltpu.SMEM)] + [block] * 4,
        out_specs=(block, block, block),
        cost_estimate=pl.CostEstimate(flops=10**6, bytes_accessed=8 << 20, transcendentals=0),
        name="update",
    )(scal, state, direction, rn, precond)


def solution(mesh):
    return jax.shard_map(
        shards,
        mesh=mesh,
        in_specs=(
            P("lat", None, "ch"), P("lat", None, "ch"), P("lat", None, "ch"), P("lat", None, "ch"),
            P("lat", "ch"), P(None, None, "lat", "ch"), P(None, "ch", None, None),
            P(None, "ch", None, None), P(None, "ch"), P("ch", None), P("ch"),
            P("lat", None, None), P("lat", None), P("lat", None, None),
        ),
        out_specs=(P("lat", None, "ch"), P("lat", None, "ch"), P("lat", None, "ch")),
        check_vma=False,
    )
```

time: 448 us -> 76.5 us (0.17); the launches traced: 440 us -> 76.1 us
  blocking collectives: 145 us -> 0 us
  waiting for transfers between devices: 91.4 us -> 0 us
  Pallas kernels: 0 us -> 73.5 us
  matrix products: 60 us -> 0 us
  local copies, waits for them, and re-layouts: 56.1 us -> 1.96 us
  starting transfers between devices: 52.4 us -> 0 us
  between operations: 20.7 us -> 0.64 us
  other arithmetic: 15.1 us -> 0 us
    psum x3 -> x0, blocking collectives: 135 us -> none  [the longest x1 66.7 us: shards(): sums = lax.psum(jnp.stack([own_now, own_curve]), ('lat', 'ch'))]
    unnamed x3 -> x0, waiting for transfers between devices: 77.1 us -> none
    pallas_call x0 -> x2, Pallas kernels: none -> 73.5 us  [the longest x1 69.2 us: shards(): pl.pallas_call(kernel, out_shape=(jax.ShapeDtypeStruct((4, 256, 256), F32...]
    dot_general x42 -> x0, matrix products: 60 us -> none  [the longest x2 7.91 us: lon_backward(): jnp.einsum('kw,lkd->lwd', sin_table, imag_part, precision=HIGH)]
    all_to_all x8 -> x0, starting transfers between devices: 52.3 us -> none  [the longest x2 14.3 us: spectral(): lax.all_to_all(real_part.astype(jnp.bfloat16), 'lat', split_axis=1, conca...]
    unnamed x69 -> x0, local copies, waits for them, and re-layouts: 21.4 us -> none
    all_to_all x14 -> x0, local copies, waits for them, and re-layouts: 19.7 us -> none  [the longest x4 5.3 us: spectral(): lax.all_to_all(imag_part.astype(jnp.bfloat16), 'lat', split_axis=1, conca...]
    all_to_all x8 -> x0, waiting for transfers between devices: 14.4 us -> none  [the longest x2 6.34 us: spectral(): lax.all_to_all(imag_part.astype(jnp.bfloat16), 'lat', split_axis=0, conca...]
  transfers between devices with their start and end apart: 10 -> 0, of which waited for: 7 -> 0; matrix products, arithmetic and copies ran while one was open for 18% -> 0% of each run, Pallas kernels for 0% -> 0%
where the time goes in v2:
time: 76.5 us; the launch traced here: 76.1 us
  Pallas kernels  73.5 us (96%)
  local copies, waits for them, and re-layouts  1.96 us (3%)
    pallas_call x1, Pallas kernels, shards(): pl.pallas_call(kernel, out_shape=(jax.ShapeDtypeStruct((4, 256, 256), F32...  69.2 us
    pallas_call x1, Pallas kernels, shards(): pl.pallas_call(finish, out_shape=(shape, shape, shape), grid=(4,), in_spe...  4.37 us
    reshape x1, local copies, waits for them, and re-layouts, shards(): spectral_slope.reshape(2, 512, 256)  1.96 us

profile of v2, /device:TPU:1, one launch (start us, length us, event | category | flops | bytes accessed | tf_op | source)
XLA Modules:
  0.0 76.1 jit_solution(13199141244456997354)
XLA Ops:
  0.6 2.0 %reshape.12.sslope_hbm = bf16[2,512,256]{2,1,0:T(8,128)(2,1)} reshape(bf16[2,128,4,256]{3,2,1,0:T(4,128)(2,1)} %param.25) | data formatting | bytes 1048576 | tf_op jit(solution)/shard_map/reshape | solution.py:492
  2.6 69.2 %spectral_step.1 = (f32[4,256,256]{2,1,0:T(8,128)}, f32[1,128]{1,0:T(1,128)}) custom-call(s32[1,4]{1,0:T(1,128)} %count_ref.1, f32[4,256,256]{2,1,0:T(8,128)} %direction.1, f32[4,256,256]{2,1,0:T(8,128)} %r_hbm.1, f32[4,256,256]{2,1,0:T(8,128)} %precond.1, bf16[1024,1024]{1,0:T(8,128)(2,1)} %slope_hbm.1, bf16[2,512,256]{2,1,0:T(8,128)(2,1)} %reshape.12.sslope_hbm, ...), custom_call_target="tpu_custom_call" | custom-call | flops 4000000000 | bytes 14680064 | tf_op jit(solution)/shard_map/spectral_step/pallas_call | solution.py:477
  71.8 4.4 %update.1 = (f32[4,256,256]{2,1,0:T(8,128)}, f32[4,256,256]{2,1,0:T(8,128)}, f32[4,256,256]{2,1,0:T(8,128)}) custom-call(f32[1,128]{1,0:T(1,128)} %get-tuple-element.5.scal, f32[4,256,256]{2,1,0:T(8,128)} %state.1, f32[4,256,256]{2,1,0:T(8,128)} %direction.1, f32[4,256,256]{2,1,0:T(8,128)} %get-tuple-element.6.rn, f32[4,256,256]{2,1,0:T(8,128)} %precond.1), custom_call_target="tpu_custom_call" | custom-call | flops 1000000 | bytes 8388608 | tf_op jit(solution)/shard_map/update/pallas_call | solution.py:497

commit v3 on v2

--- a/solution.py
+++ b/solution.py
@@ -91,11 +91,11 @@
 def kernel(
     count_ref, d_hbm, r_hbm, p_hbm, slope_hbm, sslope_hbm, fin_hbm, fout_hbm, wup_hbm, wdown_hbm,
     ow_hbm, tok_hbm, rinv_hbm, lon_hbm, back_hbm, lona_hbm, backa_hbm, mix_hbm, unmix_hbm,
-    rn_hbm, scal_ref,
+    rn_hbm,
     d, r, p, slope, sslope, fin, fout, wup, wdown, tok, rinv, lon_t, back_t, lona_t, backa_t,
-    mix_t, unmix_t, owz, sl, wk, wl, wupu, g_far, g_own, g_next, g_prev, q, qcat, esum, base,
-    spread, lat_rows, send, recv, rpart, rrecv, out_far, out_next, out_prev, out_acc,
-    in_far, in_next, in_prev, in_acc, proj, ar1, ar1z, ar2, ar2z, rn,
+    mix_t, unmix_t, owz, sl, wk, wl, wupu, g_own, g_next, g_prev, q, qcat, esum, base,
+    spread, send, recv, rpart, rrecv, out_far, out_next, out_prev, out_acc,
+    in_far, in_next, in_prev, in_acc, proj, ar1, ar1z, ar2, rn, scal,
     load_sem, a_send, a_recv, z_send, z_recv, s_send, s_recv, out_sem,
 ):
     me = lax.axis_index("lat")
@@ -116,30 +116,26 @@
             (r_hbm, r), (p_hbm, p), (lona_hbm, lona_t), (backa_hbm, backa_t),
         ])
     ]
-    for copy in loads:
+    for copy in loads[:5]:
         copy.start()
     (l_d, l_lon, l_tok, l_rinv, l_ow, l_wdown, l_wup, l_slope, l_mix, l_fin, l_fout, l_sslope,
      l_unmix, l_back, l_r, l_p, l_lona, l_backa) = loads
 
     barrier = pltpu.get_barrier_semaphore()
 
-    def greet(o, carry):
-        pl.semaphore_signal(barrier, inc=1, device_id=(peer(o), z), device_id_type=MESH)
-        return carry
-
-    lax.fori_loop(1, N_LAT, greet, 0)
+    peers = [peer(o) for o in range(1, N_LAT)]
+    for other in peers:
+        pl.semaphore_signal(barrier, inc=1, device_id=(other, z), device_id_type=MESH)
     for other in (z_next, z_prev, z_far):
         pl.semaphore_signal(barrier, inc=1, device_id=(me, other), device_id_type=MESH)
+    for copy in loads[5:]:
+        copy.start()
 
     def to_all(src_of, dst, send_sem, recv_sem):
-        def go(o, carry):
-            other = peer(o)
+        for other in peers:
             pltpu.make_async_remote_copy(
                 src_of(other), dst, send_sem, recv_sem, device_id=(other, z), device_id_type=MESH
             ).start()
-            return carry
-
-        lax.fori_loop(1, N_LAT, go, 0)
 
     def wait_for(ref, n, sem):
         part = ref.at[pl.ds(0, n)]
@@ -167,11 +163,23 @@
         rows = jnp.concatenate([rows[:, :, 128 * h:128 * h + 128] for h in range(4)], axis=1)
         send[stage * 2 + c] = rows.astype(BF)
 
+    l_ow.wait()
+    pl.semaphore_wait(barrier, N_LAT - 1 + N_CH - 1)
+
+    ow_copies = [
+        pltpu.make_async_remote_copy(
+            owz.at[z], owz.at[z], s_send.at[0], s_recv.at[0], device_id=(me, other),
+            device_id_type=MESH)
+        for other in (z_next, z_prev, z_far)
+    ]
+    for copy in ow_copies:
+        copy.start()
     l_d.wait()
     l_lon.wait()
     for c in range(2):
         x = jnp.concatenate([d[h, :, 128 * c:128 * c + 128] for h in range(4)], axis=1)
         pack_rows(0, c, dot(lon_t[...], right3(x)))
+        scatter(0, c)
 
     l_tok.wait()
     l_rinv.wait()
@@ -191,19 +199,6 @@
     spread_now = dot_nt(jnp.concatenate(where_high, axis=1), jnp.concatenate(where_low, axis=1))
     rpart[...] = spread_now.reshape(N_LAT, 8, 128)
 
-    l_ow.wait()
-    pl.semaphore_wait(barrier, N_LAT - 1 + N_CH - 1)
-
-    ow_copies = [
-        pltpu.make_async_remote_copy(
-            owz.at[z], owz.at[z], s_send.at[0], s_recv.at[0], device_id=(me, other),
-            device_id_type=MESH)
-        for other in (z_next, z_prev, z_far)
-    ]
-    for copy in ow_copies:
-        copy.start()
-    scatter(0, 0)
-    scatter(0, 1)
     rrecv[me] = rpart[me]
     to_all(lambda o: rpart.at[o], rrecv.at[me], s_send.at[1], s_recv.at[1])
 
@@ -219,31 +214,32 @@
     parts = jnp.where(sub == 0, w0.astype(F32), jnp.where(sub == 1, w1.astype(F32), jnp.where(
         sub == 2, w2.astype(F32), zero)))
     u = jnp.sum(dot_nt(parts.astype(BF), wdown[...]), axis=0, keepdims=True)
-    wupu[...] = (wup[...].astype(F32) * u).astype(BF)
-
-    def share(owner, dst):
-        cols = wupu[pl.ds(pl.multiple_of(owner * 256, 256), 256), :]
-
-        def rows(i, carry):
-            at = pl.ds(pl.multiple_of(i * 256, 256), 256)
-            dst[at, :] = dot_nt(slope[at, :], cols).astype(dst.dtype)
-            return carry
-
-        lax.fori_loop(0, 4, rows, 0)
+
+    def scaled(owner):
+        rows = wup[pl.ds(pl.multiple_of(owner * 256, 256), 256), :]
+        return (rows.astype(F32) * u).astype(BF)
+
+    def share(k, dst, at):
+        cols = wupu[k]
+        dst[at, :] = dot_nt(slope[at, :], cols).astype(dst.dtype)
 
     top, low = pl.ds(0, 512), pl.ds(512, 512)
-    share(z_far, out_far)
-    z_copies = [
-        z_copy(out_far.at[top], in_far.at[top], z_next, 0),
-        z_copy(out_far.at[low], in_far.at[low], z_prev, 1),
-    ]
-    share(z_next, g_next)
+    z_copies = []
+    wupu[0] = scaled(z_far)
+    share(0, out_far, top)
+    z_copies.append(z_copy(out_far.at[top], in_far.at[top], z_next, 0))
+    share(0, out_far, low)
+    z_copies.append(z_copy(out_far.at[low], in_far.at[low], z_prev, 1))
+    wupu[1] = scaled(z_next)
+    share(1, g_next, low)
     out_next[...] = g_next[low, :].astype(BF)
     z_copies.append(z_copy(out_next, in_next, z_next, 2))
-    share(z_prev, g_prev)
+    wupu[2] = scaled(z_prev)
+    share(2, g_prev, top)
     out_prev[...] = g_prev[top, :].astype(BF)
     z_copies.append(z_copy(out_prev, in_prev, z_prev, 3))
-    share(z, g_own)
+    share(1, g_next, top)
+    share(2, g_prev, low)
 
     l_fin.wait()
     l_fout.wait()
@@ -259,7 +255,7 @@
     l_sslope.wait()
     for part in range(2):
         for c in range(2):
-            spread[pl.ds(0, 512), :] = sslope[part, :, 128 * c:128 * c + 128].astype(F32)
+            spread[pl.ds(0, 512), :] = sslope[part, :, :, 128 * c:128 * c + 128].astype(F32).reshape(512, 128)
             for kk in range(4):
                 sl[c, 128 * kk:128 * kk + 128, 128 * part:128 * part + 128] = (
                     spread[pl.ds(kk, 128, stride=4), :]
@@ -300,6 +296,9 @@
 
     middle(0, 0, False)
     middle(0, 1, False)
+    wupu[3] = scaled(z)
+    share(3, g_own, top)
+    share(3, g_own, low)
 
     z_copies[0].wait_recv()
     z_copies[1].wait_recv()
@@ -316,7 +315,8 @@
     l_r.wait()
     l_p.wait()
     l_back.wait()
-    own_now = jnp.sum(r[...] * r[...] / p[...], keepdims=True)[0]
+    p[...] = 1.0 / p[...]
+    own_now = jnp.sum(r[...] * r[...] * p[...], keepdims=True)[0]
     own_square = jnp.sum(d[...] * d[...], keepdims=True)[0]
 
     z_copies[2].wait_recv()
@@ -393,7 +393,7 @@
     norm_now, all_curve = sums[:, 0:1], sums[:, 1:2]
     alpha = norm_now / all_curve
 
-    total = jnp.zeros((1, 1), F32)
+    total = jnp.zeros((1, 128), F32)
     for c in range(2):
         f = back(3, c, backa_t)
         at = pl.ds(128 * c, 128)
@@ -401,25 +401,27 @@
             image = base[h, :, at] + f[:, 128 * h:128 * h + 128]
             after = r[h, :, at] - alpha * image
             rn[h, :, at] = after
-            total = total + jnp.sum(after * after / p[h, :, at], keepdims=True)
-    out_copy = pltpu.make_async_copy(rn, rn_hbm, out_sem)
-    out_copy.start()
-    ar2[me] = jnp.where(lane == 0, total, 0.0)
-    to_all(lambda o: ar2.at[me], ar2.at[me], s_send.at[5], s_recv.at[5])
-    wait_for(ar2, N_LAT - 1, s_recv.at[5])
-    ar2z[z] = jnp.sum(ar2[...], axis=0)
-    two_copies = [
-        pltpu.make_async_remote_copy(
-            ar2z.at[z], ar2z.at[z], s_send.at[6], s_recv.at[6], device_id=(me, other),
-            device_id_type=MESH)
-        for other in (z_next, z_prev, z_far)
+            total = total + jnp.sum(after * after * p[h, :, at], axis=0, keepdims=True)
+    out_copies = [
+        pltpu.make_async_copy(rn.at[h], rn_hbm.at[h, pl.ds(0, 256)], out_sem.at[h]) for h in range(4)
     ]
-    for copy in two_copies:
-        copy.start()
-    wait_for(ar2z, 3, s_recv.at[6])
-    norm_next = ((ar2z[0] + ar2z[1]) + (ar2z[2] + ar2z[3]))[:, 0:1]
+    for copy in out_copies:
+        copy.start()
+    mine = me * N_CH + z
+    ar2[mine] = total
+    for oz in (0, 1, 2, 3):
+        for other in ([me] if oz else []) + peers:
+            pltpu.make_async_remote_copy(
+                ar2.at[mine], ar2.at[mine], s_send.at[5], s_recv.at[5],
+                device_id=(other, (z + oz) % 4), device_id_type=MESH,
+            ).start()
+    wait_for(ar2, N_LAT * N_CH - 1, s_recv.at[5])
+    norm_next = jnp.sum(jnp.sum(ar2[...], axis=0), axis=1, keepdims=True)
     beta = norm_next / norm_now
-    scal_ref[...] = jnp.where(lane == 0, alpha, jnp.where(lane == 1, beta, 0.0))
+    place = lax.broadcasted_iota(jnp.int32, (8, 256), 1)
+    scal[...] = jnp.where(place == 0, alpha, jnp.where(place == 1, beta, 0.0))
+    out_copies.append(pltpu.make_async_copy(scal, rn_hbm.at[0, pl.ds(256, 8)], out_sem.at[4]))
+    out_copies[-1].start()
 
     for i in range(8):
         wait_for(send.at[i], N_LAT - 1, a_send.at[i])
@@ -430,18 +432,32 @@
     wait_for(proj, 3, s_send.at[2])
     wait_for(ar1, N_LAT - 1, s_send.at[3])
     wait_for(ar1z, 3, s_send.at[4])
-    wait_for(ar2, N_LAT - 1, s_send.at[5])
-    wait_for(ar2z, 3, s_send.at[6])
-    out_copy.wait()
-
-
-def finish(scal, state, direction, rn, precond, state_out, rn_out, direction_out):
-    alpha, beta = scal[0, 0], scal[0, 1]
-    now = direction[...]
-    after = rn[...]
-    state_out[...] = state[...] + alpha * now
-    rn_out[...] = after
-    direction_out[...] = after / precond[...] + beta * now
+    wait_for(ar2, N_LAT * N_CH - 1, s_send.at[5])
+    for copy in out_copies:
+        copy.wait()
+
+
+def finish(
+    state, direction, precond, rn, state_out, rn_out, direction_out,
+    w_state, w_rn, w_direction, out_sem,
+):
+    puts = []
+
+    def put(k, i, src, dst):
+        puts.append(pltpu.make_async_copy(src.at[i], dst.at[i], out_sem.at[k, i]))
+        puts[-1].start()
+
+    alpha, beta = rn[0, 256:257, 0:1], rn[0, 256:257, 1:2]
+    for i in range(4):
+        now, after = direction[i], rn[i, 0:256, :]
+        w_rn[i] = after
+        put(0, i, w_rn, rn_out)
+        w_state[i] = state[i] + alpha * now
+        put(1, i, w_state, state_out)
+        w_direction[i] = after / precond[i] + beta * now
+        put(2, i, w_direction, direction_out)
+    for copy in puts:
+        copy.wait()
 
 
 def shards(
@@ -455,54 +471,52 @@
     vm = pltpu.VMEM
     field = vm((4, 256, 256), F32)
     scratch = [
-        field, field, field, vm((1024, 1024), BF), vm((2, 512, 256), BF),
+        field, field, field, vm((1024, 1024), BF), vm((2, 128, 4, 256), BF),
         vm((2, 2, 128, 128), F32), vm((2, 2, 128, 128), F32), vm((1024, 1024), BF),
         vm((1024, 1024), BF), vm((1, 4, 128), jnp.int32), vm((1, 4, 128), F32),
         vm((256, 768), BF), vm((256, 512), BF), vm((256, 256), F32), vm((256, 512), BF),
         vm((256, 512), BF), vm((256, 768), BF),
         vm((4, 1, 256), F32), vm((2, 512, 256), F32), vm((4, 768, 256), BF), vm((4, 256, 768), BF),
-        vm((1024, 1024), BF), vm((8, 128), F32), vm((1024, 256), F32), vm((1024, 256), F32),
+        vm((4, 256, 1024), BF), vm((1024, 256), F32), vm((1024, 256), F32),
         vm((1024, 256), F32), vm((1024, 256), F32), vm((4, 768, 256), BF), vm((1024, 128), F32),
-        field, vm((1024, 128), F32), vm((8, 128), F32),
+        field, vm((1024, 128), F32),
         vm((8, N_LAT, 32, 128), BF), vm((8, N_LAT, 32, 128), BF),
         vm((N_LAT, 8, 128), F32), vm((N_LAT, 8, 128), F32),
         vm((1024, 256), BF), vm((512, 256), BF), vm((512, 256), BF), vm((1024, 256), BF),
         vm((1024, 256), BF), vm((512, 256), BF), vm((512, 256), BF), vm((1024, 256), BF),
         vm((4, 1, 1024), F32), vm((N_LAT, 1, 128), F32), vm((4, 1, 128), F32),
-        vm((N_LAT, 1, 128), F32), vm((4, 1, 128), F32), field,
+        vm((N_LAT * N_CH, 1, 128), F32), field, vm((8, 256), F32),
         pltpu.SemaphoreType.DMA((18,)), pltpu.SemaphoreType.DMA((8,)), pltpu.SemaphoreType.DMA((8,)),
-        pltpu.SemaphoreType.DMA((6,)), pltpu.SemaphoreType.DMA((6,)), pltpu.SemaphoreType.DMA((7,)),
-        pltpu.SemaphoreType.DMA((7,)), pltpu.SemaphoreType.DMA,
+        pltpu.SemaphoreType.DMA((6,)), pltpu.SemaphoreType.DMA((6,)), pltpu.SemaphoreType.DMA((6,)),
+        pltpu.SemaphoreType.DMA((6,)), pltpu.SemaphoreType.DMA((5,)),
     ]
-    rn, scal = pl.pallas_call(
+    rn = pl.pallas_call(
         kernel,
-        out_shape=(
-            jax.ShapeDtypeStruct((4, 256, 256), F32), jax.ShapeDtypeStruct((1, 128), F32),
-        ),
+        out_shape=jax.ShapeDtypeStruct((4, 264, 256), F32),
         in_specs=[pl.BlockSpec(memory_space=pltpu.SMEM)] + [hbm] * 18,
-        out_specs=(hbm, pl.BlockSpec(memory_space=pltpu.VMEM)),
+        out_specs=hbm,
         scratch_shapes=scratch,
         compiler_params=pltpu.CompilerParams(
-            collective_id=0, has_side_effects=True, vmem_limit_bytes=56 << 20
+            collective_id=0, has_side_effects=True, vmem_limit_bytes=58 << 20
         ),
         cost_estimate=pl.CostEstimate(flops=4 * 10**9, bytes_accessed=14 << 20, transcendentals=0),
         name="spectral_step",
     )(
         obs_count, direction, residual, precond, token_slope,
-        spectral_slope.reshape(2, 512, 256), filter_in, filter_out, w_up, w_down,
+        spectral_slope, filter_in, filter_out, w_up, w_down,
         obs_weight.reshape(1, 256), obs_token, obs_rinv, *tables,
     )
-    block = pl.BlockSpec((1, 256, 256), lambda i: (i, 0, 0))
     shape = jax.ShapeDtypeStruct((4, 256, 256), F32)
     return pl.pallas_call(
         finish,
         out_shape=(shape, shape, shape),
-        grid=(4,),
-        in_specs=[pl.BlockSpec(memory_space=pltpu.SMEM)] + [block] * 4,
-        out_specs=(block, block, block),
-        cost_estimate=pl.CostEstimate(flops=10**6, bytes_accessed=8 << 20, transcendentals=0),
+        in_specs=[pl.BlockSpec(memory_space=pltpu.VMEM)] * 4,
+        out_specs=(hbm, hbm, hbm),
+        scratch_shapes=[field] * 3 + [pltpu.SemaphoreType.DMA((3, 4))],
+        compiler_params=pltpu.CompilerParams(vmem_limit_bytes=24 << 20),
+        cost_estimate=pl.CostEstimate(flops=10**6, bytes_accessed=7 << 20, transcendentals=0),
         name="update",
-    )(scal, state, direction, rn, precond)
+    )(state, direction, precond, rn)
 
 
 def solution(mesh):

time: 76.5 us -> 68.8 us (0.90)
  Pallas kernels: 73.5 us -> 66.7 us
    pallas_call x2, Pallas kernels: 73.5 us -> 66.7 us  [the longest x1 64.9 us: shards(): pl.pallas_call(kernel, out_shape=jax.ShapeDtypeStruct((4, 264, 256), F32)...]
    reshape x1 -> x0, local copies, waits for them, and re-layouts: 1.96 us -> none  [shards(): spectral_slope.reshape(2, 512, 256)]
    unnamed x0 -> x8, local copies, waits for them, and re-layouts: none -> 1.24 us
where the time goes in v3:
time: 68.8 us; the launch traced here: 68.6 us
  Pallas kernels  66.7 us (97%)
  local copies, waits for them, and re-layouts  1.24 us (2%)
  between operations  0.7 us (1%)
    pallas_call x1, Pallas kernels, shards(): pl.pallas_call(kernel, out_shape=jax.ShapeDtypeStruct((4, 264, 256), F32)...  64.9 us
    pallas_call x1, Pallas kernels, shards(): pl.pallas_call(finish, out_shape=(shape, shape, shape), in_specs=[pl.Bloc...  1.81 us

profile of v3, /device:TPU:1, one launch (start us, length us, event | category | flops | bytes accessed | tf_op | source)
XLA Modules:
  0.0 68.6 jit_solution(2906138446318095958)
XLA Ops:
  0.6 0.0 copy-start.1
  0.6 0.0 copy-start.2
  0.7 0.0 copy-start.3
  0.7 64.9 %spectral_step.1.rn = f32[4,264,256]{2,1,0:T(8,128)} custom-call(s32[1,4]{1,0:T(1,128)} %count_ref.1, f32[4,256,256]{2,1,0:T(8,128)} %direction.1, f32[4,256,256]{2,1,0:T(8,128)} %r_hbm.1, f32[4,256,256]{2,1,0:T(8,128)} %precond.1, bf16[1024,1024]{1,0:T(8,128)(2,1)} %slope_hbm.1, bf16[2,128,4,256]{3,2,1,0:T(4,128)(2,1)} %sslope_hbm.1, ...), custom_call_target="tpu_custom_call" | custom-call | flops 4000000000 | bytes 14680064 | tf_op jit(solution)/shard_map/spectral_step/pallas_call | solution.py:493
  65.5 0.0 copy-done.1
  65.5 0.0 copy-done.2
  65.5 0.0 copy-done.3
  65.6 0.0 copy-start
  65.6 1.2 %copy-done = f32[4,264,256]{2,1,0:T(8,128)S(1)} copy-done((f32[4,264,256]{2,1,0:T(8,128)S(1)}, f32[4,264,256]{2,1,0:T(8,128)}, u32[]{:S(2)}) %copy-start) | copy-done | bytes 1081368
  66.8 1.8 %update.1 = (f32[4,256,256]{2,1,0:T(8,128)}, f32[4,256,256]{2,1,0:T(8,128)}, f32[4,256,256]{2,1,0:T(8,128)}) custom-call(f32[4,256,256]{2,1,0:T(8,128)S(1)} %copy-done.1, f32[4,256,256]{2,1,0:T(8,128)S(1)} %copy-done.2, f32[4,256,256]{2,1,0:T(8,128)S(1)} %copy-done.3, f32[4,264,256]{2,1,0:T(8,128)S(1)} %copy-done), custom_call_target="tpu_custom_call" | custom-call | flops 1000000 | bytes 7340032 | tf_op jit(solution)/shard_map/update/pallas_call | solution.py:510
Async XLA Ops:
  0.6 64.9 %copy-start.1 = (f32[4,256,256]{2,1,0:T(8,128)S(1)}, f32[4,256,256]{2,1,0:T(8,128)}, u32[]{:S(2)}) copy-start(f32[4,256,256]{2,1,0:T(8,128)} %state.1) | copy-start | bytes 3145732
  0.6 64.9 %copy-start.2 = (f32[4,256,256]{2,1,0:T(8,128)S(1)}, f32[4,256,256]{2,1,0:T(8,128)}, u32[]{:S(2)}) copy-start(f32[4,256,256]{2,1,0:T(8,128)} %direction.1) | copy-start | bytes 3145732
  0.7 64.9 %copy-start.3 = (f32[4,256,256]{2,1,0:T(8,128)S(1)}, f32[4,256,256]{2,1,0:T(8,128)}, u32[]{:S(2)}) copy-start(f32[4,256,256]{2,1,0:T(8,128)} %precond.1) | copy-start | bytes 3145732
  65.6 1.2 %copy-start = (f32[4,264,256]{2,1,0:T(8,128)S(1)}, f32[4,264,256]{2,1,0:T(8,128)}, u32[]{:S(2)}) copy-start(f32[4,264,256]{2,1,0:T(8,128)} %spectral_step.1.rn) | copy-start | bytes 3244036

commit v4 on v3

--- a/solution.py
+++ b/solution.py
@@ -93,7 +93,7 @@
     ow_hbm, tok_hbm, rinv_hbm, lon_hbm, back_hbm, lona_hbm, backa_hbm, mix_hbm, unmix_hbm,
     rn_hbm,
     d, r, p, slope, sslope, fin, fout, wup, wdown, tok, rinv, lon_t, back_t, lona_t, backa_t,
-    mix_t, unmix_t, owz, sl, wk, wl, wupu, g_own, g_next, g_prev, q, qcat, esum, base,
+    mix_t, unmix_t, owz, sl, wk, wl, wupu, g_own, g_next, g_prev, q, qcat, base,
     spread, send, recv, rpart, rrecv, out_far, out_next, out_prev, out_acc,
     in_far, in_next, in_prev, in_acc, proj, ar1, ar1z, ar2, rn, scal,
     load_sem, a_send, a_recv, z_send, z_recv, s_send, s_recv, out_sem,
@@ -106,6 +106,18 @@
     def peer(o):
         dx, dy, dc = o // 8, (o // 2) % 4, o % 2
         return ((px + dx) % 4) * 8 + ((py + dy) % 4) * 2 + (pc + dc) % 2
+
+    barrier = pltpu.get_barrier_semaphore()
+
+    def hops(o):
+        dx, dy, dc = o // 8, (o // 2) % 4, o % 2
+        return min(dx, 4 - dx) + min(dy, 4 - dy) + dc / 4
+
+    peers = [peer(o) for o in sorted(range(1, N_LAT), key=hops, reverse=True)]
+    for other in peers:
+        pl.semaphore_signal(barrier, inc=1, device_id=(other, z), device_id_type=MESH)
+    for other in (z_next, z_prev, z_far):
+        pl.semaphore_signal(barrier, inc=1, device_id=(me, other), device_id_type=MESH)
 
     loads = [
         pltpu.make_async_copy(src, dst, load_sem.at[i])
@@ -121,13 +133,6 @@
     (l_d, l_lon, l_tok, l_rinv, l_ow, l_wdown, l_wup, l_slope, l_mix, l_fin, l_fout, l_sslope,
      l_unmix, l_back, l_r, l_p, l_lona, l_backa) = loads
 
-    barrier = pltpu.get_barrier_semaphore()
-
-    peers = [peer(o) for o in range(1, N_LAT)]
-    for other in peers:
-        pl.semaphore_signal(barrier, inc=1, device_id=(other, z), device_id_type=MESH)
-    for other in (z_next, z_prev, z_far):
-        pl.semaphore_signal(barrier, inc=1, device_id=(me, other), device_id_type=MESH)
     for copy in loads[5:]:
         copy.start()
 
@@ -296,9 +301,6 @@
 
     middle(0, 0, False)
     middle(0, 1, False)
-    wupu[3] = scaled(z)
-    share(3, g_own, top)
-    share(3, g_own, low)
 
     z_copies[0].wait_recv()
     z_copies[1].wait_recv()
@@ -307,6 +309,9 @@
     out_acc[low, :] = (g_prev[low, :] + in_far[low, :].astype(F32)).astype(BF)
     acc_prev = z_copy(out_acc.at[low], in_acc.at[low], z_prev, 5)
     z_copies += [acc_next, acc_prev]
+    wupu[3] = scaled(z)
+    share(3, g_own, top)
+    share(3, g_own, low)
 
     wait_for(rrecv, N_LAT - 1, s_recv.at[1])
     rsum = jnp.sum(rrecv[...], axis=0)
@@ -319,30 +324,24 @@
     own_now = jnp.sum(r[...] * r[...] * p[...], keepdims=True)[0]
     own_square = jnp.sum(d[...] * d[...], keepdims=True)[0]
 
+    for c in range(2):
+        f = back(1, c, back_t)
+        at = pl.ds(128 * c, 128)
+        for h in range(4):
+            base[h, :, at] = d[h, :, at] + f[:, 128 * h:128 * h + 128]
+
     z_copies[2].wait_recv()
     z_copies[3].wait_recv()
     acc_next.wait_recv()
     acc_prev.wait_recv()
     own_weight = owz[z]
-    q_top = g_own[top, :] + in_acc[top, :].astype(F32) + in_prev[...].astype(F32) + own_weight
-    q_low = g_own[low, :] + in_acc[low, :].astype(F32) + in_next[...].astype(F32) + own_weight
-    q[top, :] = q_top
-    q[low, :] = q_low
-    for h in range(4):
-        high, low_part = split(q[256 * h:256 * h + 256, :])
-        qcat[h] = jnp.concatenate([high, high, low_part], axis=0)
-
-    for c in range(2):
-        f = back(1, c, back_t)
-        at = pl.ds(128 * c, 128)
-        for h in range(4):
-            rows = pl.ds(256 * h, 256)
-            e = (d[h, :, at] + f[:, 128 * h:128 * h + 128]) * q[rows, at]
-            if c == 0:
-                esum[rows, :] = e
-            else:
-                esum[rows, :] = esum[rows, :] + e
-    ehigh, elow = split(esum[...])
+    sums = []
+    for at, direct, first in ((top, in_prev, 0), (low, in_next, 2)):
+        value = g_own[at, :] + in_acc[at, :].astype(F32) + direct[...].astype(F32) + own_weight
+        q[at, :] = value
+        e = base[pl.ds(first, 2)].reshape(512, 256) * value
+        sums.append(e[:, 0:128] + e[:, 128:256])
+    ehigh, elow = split(jnp.concatenate(sums, axis=0))
     mine = dot_nt(jnp.ones((8, 256), BF), jnp.concatenate([ehigh, elow], axis=1))
     proj[z] = mine[0:1, :]
     p_copies = [
@@ -353,6 +352,8 @@
     ]
     for copy in p_copies:
         copy.start()
+    for h in range(4):
+        qcat[h] = right3(q[256 * h:256 * h + 256, :])
     l_lona.wait()
     l_backa.wait()
     wait_for(proj, 3, s_recv.at[2])
@@ -409,20 +410,12 @@
         copy.start()
     mine = me * N_CH + z
     ar2[mine] = total
-    for oz in (0, 1, 2, 3):
-        for other in ([me] if oz else []) + peers:
+    for oz in (2, 1, 3, 0):
+        for other in peers + ([me] if oz else []):
             pltpu.make_async_remote_copy(
                 ar2.at[mine], ar2.at[mine], s_send.at[5], s_recv.at[5],
                 device_id=(other, (z + oz) % 4), device_id_type=MESH,
             ).start()
-    wait_for(ar2, N_LAT * N_CH - 1, s_recv.at[5])
-    norm_next = jnp.sum(jnp.sum(ar2[...], axis=0), axis=1, keepdims=True)
-    beta = norm_next / norm_now
-    place = lax.broadcasted_iota(jnp.int32, (8, 256), 1)
-    scal[...] = jnp.where(place == 0, alpha, jnp.where(place == 1, beta, 0.0))
-    out_copies.append(pltpu.make_async_copy(scal, rn_hbm.at[0, pl.ds(256, 8)], out_sem.at[4]))
-    out_copies[-1].start()
-
     for i in range(8):
         wait_for(send.at[i], N_LAT - 1, a_send.at[i])
     for copy in z_copies:
@@ -432,6 +425,14 @@
     wait_for(proj, 3, s_send.at[2])
     wait_for(ar1, N_LAT - 1, s_send.at[3])
     wait_for(ar1z, 3, s_send.at[4])
+    wait_for(ar2, N_LAT * N_CH - 1, s_recv.at[5])
+    norm_next = jnp.sum(jnp.sum(ar2[...], axis=0), axis=1, keepdims=True)
+    beta = norm_next / norm_now
+    place = lax.broadcasted_iota(jnp.int32, (8, 256), 1)
+    scal[...] = jnp.where(place == 0, alpha, jnp.where(place == 1, beta, 0.0))
+    out_copies.append(pltpu.make_async_copy(scal, rn_hbm.at[0, pl.ds(256, 8)], out_sem.at[4]))
+    out_copies[-1].start()
+
     wait_for(ar2, N_LAT * N_CH - 1, s_send.at[5])
     for copy in out_copies:
         copy.wait()
@@ -478,7 +479,7 @@
         vm((256, 512), BF), vm((256, 768), BF),
         vm((4, 1, 256), F32), vm((2, 512, 256), F32), vm((4, 768, 256), BF), vm((4, 256, 768), BF),
         vm((4, 256, 1024), BF), vm((1024, 256), F32), vm((1024, 256), F32),
-        vm((1024, 256), F32), vm((1024, 256), F32), vm((4, 768, 256), BF), vm((1024, 128), F32),
+        vm((1024, 256), F32), vm((1024, 256), F32), vm((4, 768, 256), BF),
         field, vm((1024, 128), F32),
         vm((8, N_LAT, 32, 128), BF), vm((8, N_LAT, 32, 128), BF),
         vm((N_LAT, 8, 128), F32), vm((N_LAT, 8, 128), F32),

time: 68.8 us -> 66.3 us (0.964)
  Pallas kernels: 66.7 us -> 64.2 us
    pallas_call x1, Pallas kernels: 64.9 us -> 62.4 us  [shards(): pl.pallas_call(kernel, out_shape=jax.ShapeDtypeStruct((4, 264, 256), F32)...]
where the time goes in v4:
time: 66.3 us; the launch traced here: 66.2 us
  Pallas kernels  64.2 us (97%)
  local copies, waits for them, and re-layouts  1.24 us (2%)
  between operations  0.7 us (1%)
    pallas_call x1, Pallas kernels, shards(): pl.pallas_call(kernel, out_shape=jax.ShapeDtypeStruct((4, 264, 256), F32)...  62.4 us
    pallas_call x1, Pallas kernels, shards(): pl.pallas_call(finish, out_shape=(shape, shape, shape), in_specs=[pl.Bloc...  1.81 us

profile of v4, /device:TPU:1, one launch (start us, length us, event | category | flops | bytes accessed | tf_op | source)
XLA Modules:
  0.0 66.2 jit_solution(6938092713095051785)
XLA Ops:
  0.6 0.0 copy-start.1
  0.6 0.0 copy-start.2
  0.7 0.0 copy-start.3
  0.7 62.4 %spectral_step.1.rn = f32[4,264,256]{2,1,0:T(8,128)} custom-call(s32[1,4]{1,0:T(1,128)} %count_ref.1, f32[4,256,256]{2,1,0:T(8,128)} %direction.1, f32[4,256,256]{2,1,0:T(8,128)} %r_hbm.1, f32[4,256,256]{2,1,0:T(8,128)} %precond.1, bf16[1024,1024]{1,0:T(8,128)(2,1)} %slope_hbm.1, bf16[2,128,4,256]{3,2,1,0:T(4,128)(2,1)} %sslope_hbm.1, ...), custom_call_target="tpu_custom_call" | custom-call | flops 4000000000 | bytes 14680064 | tf_op jit(solution)/shard_map/spectral_step/pallas_call | solution.py:494
  63.1 0.0 copy-done.1
  63.1 0.0 copy-done.2
  63.1 0.0 copy-done.3
  63.1 0.0 copy-start
  63.1 1.2 %copy-done = f32[4,264,256]{2,1,0:T(8,128)S(1)} copy-done((f32[4,264,256]{2,1,0:T(8,128)S(1)}, f32[4,264,256]{2,1,0:T(8,128)}, u32[]{:S(2)}) %copy-start) | copy-done | bytes 1081368
  64.4 1.8 %update.1 = (f32[4,256,256]{2,1,0:T(8,128)}, f32[4,256,256]{2,1,0:T(8,128)}, f32[4,256,256]{2,1,0:T(8,128)}) custom-call(f32[4,256,256]{2,1,0:T(8,128)S(1)} %copy-done.1, f32[4,256,256]{2,1,0:T(8,128)S(1)} %copy-done.2, f32[4,256,256]{2,1,0:T(8,128)S(1)} %copy-done.3, f32[4,264,256]{2,1,0:T(8,128)S(1)} %copy-done), custom_call_target="tpu_custom_call" | custom-call | flops 1000000 | bytes 7340032 | tf_op jit(solution)/shard_map/update/pallas_call | solution.py:511
Async XLA Ops:
  0.6 62.5 %copy-start.1 = (f32[4,256,256]{2,1,0:T(8,128)S(1)}, f32[4,256,256]{2,1,0:T(8,128)}, u32[]{:S(2)}) copy-start(f32[4,256,256]{2,1,0:T(8,128)} %state.1) | copy-start | bytes 3145732
  0.6 62.5 %copy-start.2 = (f32[4,256,256]{2,1,0:T(8,128)S(1)}, f32[4,256,256]{2,1,0:T(8,128)}, u32[]{:S(2)}) copy-start(f32[4,256,256]{2,1,0:T(8,128)} %direction.1) | copy-start | bytes 3145732
  0.7 62.5 %copy-start.3 = (f32[4,256,256]{2,1,0:T(8,128)S(1)}, f32[4,256,256]{2,1,0:T(8,128)}, u32[]{:S(2)}) copy-start(f32[4,256,256]{2,1,0:T(8,128)} %precond.1) | copy-start | bytes 3145732
  63.1 1.2 %copy-start = (f32[4,264,256]{2,1,0:T(8,128)S(1)}, f32[4,264,256]{2,1,0:T(8,128)}, u32[]{:S(2)}) copy-start(f32[4,264,256]{2,1,0:T(8,128)} %spectral_step.1.rn) | copy-start | bytes 3244036

commit v5 on v4

--- a/solution.py
+++ b/solution.py
@@ -439,23 +439,30 @@
 
 
 def finish(
-    state, direction, precond, rn, state_out, rn_out, direction_out,
-    w_state, w_rn, w_direction, out_sem,
+    state, direction, precond, rn_hbm, state_out, rn_out, direction_out,
+    rn, scal, w_state, w_direction, in_sem, out_sem,
 ):
+    gets = [pltpu.make_async_copy(rn_hbm.at[0, pl.ds(256, 8)], scal, in_sem.at[4])]
+    gets += [
+        pltpu.make_async_copy(rn_hbm.at[i, pl.ds(0, 256)], rn.at[i], in_sem.at[i]) for i in range(4)
+    ]
+    for copy in gets:
+        copy.start()
     puts = []
 
     def put(k, i, src, dst):
         puts.append(pltpu.make_async_copy(src.at[i], dst.at[i], out_sem.at[k, i]))
         puts[-1].start()
 
-    alpha, beta = rn[0, 256:257, 0:1], rn[0, 256:257, 1:2]
+    gets[0].wait()
+    alpha, beta = scal[0:1, 0:1], scal[0:1, 1:2]
     for i in range(4):
-        now, after = direction[i], rn[i, 0:256, :]
-        w_rn[i] = after
-        put(0, i, w_rn, rn_out)
-        w_state[i] = state[i] + alpha * now
-        put(1, i, w_state, state_out)
-        w_direction[i] = after / precond[i] + beta * now
+        w_state[i] = state[i] + alpha * direction[i]
+        put(0, i, w_state, state_out)
+    for i in range(4):
+        gets[1 + i].wait()
+        put(1, i, rn, rn_out)
+        w_direction[i] = rn[i] / precond[i] + beta * direction[i]
         put(2, i, w_direction, direction_out)
     for copy in puts:
         copy.wait()
@@ -493,7 +500,7 @@
     ]
     rn = pl.pallas_call(
         kernel,
-        out_shape=jax.ShapeDtypeStruct((4, 264, 256), F32),
+        out_shape=jax.ShapeDtypeStruct((112, 264, 256), F32),
         in_specs=[pl.BlockSpec(memory_space=pltpu.SMEM)] + [hbm] * 18,
         out_specs=hbm,
         scratch_shapes=scratch,
@@ -511,10 +518,12 @@
     return pl.pallas_call(
         finish,
         out_shape=(shape, shape, shape),
-        in_specs=[pl.BlockSpec(memory_space=pltpu.VMEM)] * 4,
+        in_specs=[pl.BlockSpec(memory_space=pltpu.VMEM)] * 3 + [hbm],
         out_specs=(hbm, hbm, hbm),
-        scratch_shapes=[field] * 3 + [pltpu.SemaphoreType.DMA((3, 4))],
-        compiler_params=pltpu.CompilerParams(vmem_limit_bytes=24 << 20),
+        scratch_shapes=[field, vm((8, 256), F32), field, field] + [
+            pltpu.SemaphoreType.DMA((5,)), pltpu.SemaphoreType.DMA((3, 4)),
+        ],
+        compiler_params=pltpu.CompilerParams(vmem_limit_bytes=40 << 20),
         cost_estimate=pl.CostEstimate(flops=10**6, bytes_accessed=7 << 20, transcendentals=0),
         name="update",
     )(state, direction, precond, rn)

time: 66.3 us -> 65.9 us (level)
  local copies, waits for them, and re-layouts: 1.24 us -> 0.01 us
  Pallas kernels: 64.2 us -> 65 us
    unnamed x8 -> x6, local copies, waits for them, and re-layouts: 1.24 us -> 0.01 us
    pallas_call x1, Pallas kernels: 1.81 us -> 2.6 us  [shards(): pl.pallas_call(finish, out_shape=(shape, shape, shape), in_specs=[pl.Bloc...]
where the time goes in v5:
time: 65.9 us; the launch traced here: 65.7 us
  Pallas kernels  65 us (99%)
  between operations  0.69 us (1%)
    pallas_call x1, Pallas kernels, shards(): pl.pallas_call(kernel, out_shape=jax.ShapeDtypeStruct((112, 264, 256), F3...  62.4 us
    pallas_call x1, Pallas kernels, shards(): pl.pallas_call(finish, out_shape=(shape, shape, shape), in_specs=[pl.Bloc...  2.6 us

profile of v5, /device:TPU:1, one launch (start us, length us, event | category | flops | bytes accessed | tf_op | source)
XLA Modules:
  0.0 65.7 jit_solution(8590820058444730167)
XLA Ops:
  0.6 0.0 copy-start
  0.6 0.0 copy-start.1
  0.7 0.0 copy-start.2
  0.7 62.4 %spectral_step.1.rn_hbm = f32[112,264,256]{2,1,0:T(8,128)} custom-call(s32[1,4]{1,0:T(1,128)} %count_ref.1, f32[4,256,256]{2,1,0:T(8,128)} %direction.1, f32[4,256,256]{2,1,0:T(8,128)} %r_hbm.1, f32[4,256,256]{2,1,0:T(8,128)} %precond.1, bf16[1024,1024]{1,0:T(8,128)(2,1)} %slope_hbm.1, bf16[2,128,4,256]{3,2,1,0:T(4,128)(2,1)} %sslope_hbm.1, ...), custom_call_target="tpu_custom_call" | custom-call | flops 4000000000 | bytes 14680064 | tf_op jit(solution)/shard_map/spectral_step/pallas_call | solution.py:501
  63.1 0.0 copy-done
  63.1 0.0 copy-done.1
  63.1 0.0 copy-done.2
  63.1 2.6 %update.1 = (f32[4,256,256]{2,1,0:T(8,128)}, f32[4,256,256]{2,1,0:T(8,128)}, f32[4,256,256]{2,1,0:T(8,128)}) custom-call(f32[4,256,256]{2,1,0:T(8,128)S(1)} %copy-done.2, f32[4,256,256]{2,1,0:T(8,128)S(1)} %copy-done, f32[4,256,256]{2,1,0:T(8,128)S(1)} %copy-done.1, f32[112,264,256]{2,1,0:T(8,128)} %spectral_step.1.rn_hbm), custom_call_target="tpu_custom_call" | custom-call | flops 1000000 | bytes 7340032 | tf_op jit(solution)/shard_map/update/pallas_call | solution.py:518
Async XLA Ops:
  0.6 62.5 %copy-start = (f32[4,256,256]{2,1,0:T(8,128)S(1)}, f32[4,256,256]{2,1,0:T(8,128)}, u32[]{:S(2)}) copy-start(f32[4,256,256]{2,1,0:T(8,128)} %direction.1) | copy-start | bytes 3145732
  0.6 62.5 %copy-start.1 = (f32[4,256,256]{2,1,0:T(8,128)S(1)}, f32[4,256,256]{2,1,0:T(8,128)}, u32[]{:S(2)}) copy-start(f32[4,256,256]{2,1,0:T(8,128)} %precond.1) | copy-start | bytes 3145732
  0.7 62.5 %copy-start.2 = (f32[4,256,256]{2,1,0:T(8,128)S(1)}, f32[4,256,256]{2,1,0:T(8,128)}, u32[]{:S(2)}) copy-start(f32[4,256,256]{2,1,0:T(8,128)} %state.1) | copy-start | bytes 3145732
